TPU v7x, 32 devices: a whole 2x2x4 slice. The times are simulated.
32 devices in a mesh: groups: 2 (over y), gx: 4 (over x, core), gy: 4 (over z).
Axes of the slice: x: 2, y: 2, z: 4, core: 2. Of those that a mesh axis runs over, the one named last changes fastest.
Arguments:
- theta: float32 [32, 128, 512], P('groups', 'gx', 'gy'), parts along dimension 0, may hold values from -6 to 6
- terrain: float32 [256, 512], P(('groups', 'gx'), 'gy'), parts along dimension 0, may hold values from 0.5 to 2
- head: float32 [16, 256, 1024], P('groups', 'gy', 'gx'), parts along dimension 0, may hold values from -5 to -0.1
- soil: int32 [512, 1024], P(('groups', 'gy'), 'gx'), parts along dimension 0, may hold values from 0 to 7
- pair_map: int32 [8, 2], replicated, may hold values from 0 to 3
- tiles: float32 [8, 2, 128, 128], replicated, may hold values from -0.375 to 0.375
- vg_alpha: float32 [8], replicated, may hold values from 0.5 to 4
- vg_n: float32 [8], replicated, may hold values from 1.3 to 3
- ksat: float32 [8], replicated, may hold values from 0.05 to 1
Outputs:
- theta_next: float32 [32, 128, 512], P('groups', 'gx', 'gy'), parts along dimension 0
- head_next: float32 [16, 256, 1024], P('groups', 'gy', 'gx'), parts along dimension 0
There are 2 independent parts, one for each index of `groups`. A program takes and returns all parts, laid end to end along the dimension named above; an argument that names none is the same for every part. Nothing has to cross between parts.
All inputs are finite; a program needn't handle non-finite values.
Results may differ from a plain program's by a relative error of at most 0.00014.
Values sent between devices are 32-bit elements; how exact they have to be, the bound alone decides.
A program may use at most 64 MiB of HBM per device.

v0:
```python
import jax
import jax.numpy as jnp
from jax import lax
from jax.sharding import PartitionSpec as P

ITERS = 3
NSWEEP = 2


diffuse = 0.08
vertical_mix = 0.1
time_step = 4.0
infiltrate = 0.5
evaporate = 1.0
storage = 0.1


def padded_2(block, sides, width):
    for axis, dim in sides:
        count = lax.axis_size(axis)
        forward = [(i, i + 1) for i in range(count - 1)]
        backward = [(target, source) for source, target in forward]
        low = lax.ppermute(
            lax.slice_in_dim(block, block.shape[dim] - width, None, axis=dim), axis, forward
        )
        high = lax.ppermute(lax.slice_in_dim(block, 0, width, axis=dim), axis, backward)
        block = jnp.concatenate([low, block, high], axis=dim)
    return block


def local_down(rows, map_local, tiles_local):
    width = tiles_local.shape[2]
    nblock = rows.shape[1] // width
    blocks = rows.reshape(rows.shape[0], nblock, width)
    chosen = jnp.take(blocks, map_local, axis=1)
    result = jnp.einsum("rsqa,sqab->rsb", chosen, tiles_local, precision=lax.Precision.HIGHEST)
    return jnp.repeat(result.reshape(rows.shape[0], -1), 2, axis=0)


def local_up(field, map_local, tiles_local, nblock):
    width = tiles_local.shape[2]
    paired = field.reshape(field.shape[0] // 2, 2, field.shape[1])
    halves = 0.5 * (paired[:, 0] + paired[:, 1])
    blocks = halves.reshape(halves.shape[0], tiles_local.shape[0], width)
    contrib = jnp.einsum("rsb,sqab->rsqa", blocks, tiles_local, precision=lax.Precision.HIGHEST)
    onehot = (map_local[:, :, None] == jnp.arange(nblock, dtype=jnp.int32)[None, None, :]).astype(
        jnp.float32
    )
    result = jnp.einsum("rsqa,sqn->rna", contrib, onehot, precision=lax.Precision.HIGHEST)
    return result.reshape(halves.shape[0], nblock * width)


def soil_tables(soil, vg_alpha, vg_n, ksat):
    kinds = jnp.arange(vg_alpha.shape[0], dtype=jnp.int32)
    shape = (-1,) + (1,) * soil.ndim
    match = (soil[None] == kinds.reshape(shape)).astype(jnp.float32)
    alpha = jnp.sum(match * vg_alpha.reshape(shape), axis=0)
    expo = jnp.sum(match * vg_n.reshape(shape), axis=0)
    kmax = jnp.sum(match * ksat.reshape(shape), axis=0)
    return (alpha, expo, kmax)


def soil_state(head, alpha, expo, kmax):
    expo_m = 1.0 - 1.0 / expo
    sat = (1.0 + (alpha * jnp.abs(head)) ** expo) ** (-expo_m)
    inner = 1.0 - (1.0 - sat ** (1.0 / expo_m)) ** expo_m
    return (sat, kmax * jnp.sqrt(sat) * inner * inner)


def face_coeffs(padded):
    centre = padded[1:-1, 1:-1, 1:-1]
    return (
        jnp.sqrt(centre * padded[2:, 1:-1, 1:-1]),
        jnp.sqrt(centre * padded[:-2, 1:-1, 1:-1]),
        jnp.sqrt(centre * padded[1:-1, 2:, 1:-1]),
        jnp.sqrt(centre * padded[1:-1, :-2, 1:-1]),
        jnp.sqrt(centre * padded[1:-1, 1:-1, 2:]),
        jnp.sqrt(centre * padded[1:-1, 1:-1, :-2]),
    )


def apply_faces(faces, padded):
    centre = padded[1:-1, 1:-1, 1:-1]
    total = faces[0] * (centre - padded[2:, 1:-1, 1:-1]) + faces[1] * (
        centre - padded[:-2, 1:-1, 1:-1]
    )
    total = (
        total
        + faces[2] * (centre - padded[1:-1, 2:, 1:-1])
        + faces[3] * (centre - padded[1:-1, :-2, 1:-1])
    )
    total = (
        total
        + faces[4] * (centre - padded[1:-1, 1:-1, 2:])
        + faces[5] * (centre - padded[1:-1, 1:-1, :-2])
    )
    return total


def pad_levels(field):
    return jnp.pad(field, ((1, 1), (0, 0), (0, 0)))


def advance(padded, metric):
    centre = padded[:, 1:-1, 1:-1]
    flat = (
        padded[:, 2:, 1:-1]
        + padded[:, :-2, 1:-1]
        + padded[:, 1:-1, 2:]
        + padded[:, 1:-1, :-2]
        - 4.0 * centre
    )
    column = jnp.pad(centre, ((1, 1), (0, 0), (0, 0)))
    vert = column[2:] + column[:-2] - 2.0 * centre
    return centre + diffuse * metric * flat + vertical_mix * vert


def slab_operator(vector, faces, capacity):
    padded = pad_levels(padded_2(vector, (("gx", 2), ("gy", 1)), 1))
    return capacity * vector + apply_faces(faces, padded)


def squares_sum(vector):
    return lax.psum(jnp.sum(vector * vector), ("gx", "gy"))


def shards(theta, terrain, head, soil, pair_map, tiles, vg_alpha, vg_n, ksat):
    width = tiles.shape[2]
    slab_cols = head.shape[2]
    tile_count = slab_cols // width
    tile_start = lax.axis_index("gx") * tile_count
    map_local = lax.dynamic_slice_in_dim(pair_map, tile_start, tile_count, 0)
    tiles_local = lax.dynamic_slice_in_dim(tiles, tile_start, tile_count, 0)
    atmos_blocks = theta.shape[2] * lax.axis_size("gy") // width
    all_rows = lax.all_gather(theta[0], "gx", axis=0, tiled=True)
    bottom = lax.all_to_all(all_rows, "gy", split_axis=0, concat_axis=1, tiled=True)
    infil = local_down(bottom, map_local, tiles_local)
    alpha, expo, kmax = soil_tables(soil, vg_alpha, vg_n, ksat)
    sat, cond = soil_state(head, alpha[None], expo[None], kmax[None])
    capacity = (storage + sat) / time_step
    both = padded_2(jnp.stack([cond, head]), (("gx", 3), ("gy", 2)), 1)
    cond_pad = pad_levels(both[0])
    head_pad = pad_levels(both[1])
    faces = face_coeffs(cond_pad)
    rhs = faces[0] - faces[1] - apply_faces(faces, head_pad)
    rhs = rhs.at[0].add(infiltrate * infil)
    delta = jnp.zeros_like(head)
    resid = rhs
    direction = rhs
    norm_now = squares_sum(resid)
    for step in range(ITERS):
        image = slab_operator(direction, faces, capacity)
        alpha_step = norm_now / lax.psum(jnp.sum(direction * image), ("gx", "gy"))
        delta = delta + alpha_step * direction
        if step + 1 < ITERS:
            resid = resid - alpha_step * image
            norm_next = squares_sum(resid)
            direction = resid + norm_next / norm_now * direction
            norm_now = norm_next
    head_next = head + delta
    moist, unused = soil_state(head_next[0], alpha, expo, kmax)
    back_terms = local_up(moist, map_local, tiles_local, atmos_blocks)
    back_cols = lax.all_to_all(back_terms, "gy", split_axis=1, concat_axis=0, tiled=True)
    back = lax.psum_scatter(back_cols, "gx", scatter_dimension=0, tiled=True)
    swept = theta
    for sweep in range(NSWEEP):
        padded = padded_2(swept, (("gx", 1), ("gy", 2)), 1)
        swept = advance(padded, terrain)
    theta_next = swept.at[0].add(evaporate * back)
    return (theta_next, head_next)


def solution(mesh):
    placed = (
        P("groups", "gx", "gy"),
        P(("groups", "gx"), "gy"),
        P("groups", "gy", "gx"),
        P(("groups", "gy"), "gx"),
        P(),
        P(),
        P(),
        P(),
        P(),
    )
    return jax.shard_map(
        shards,
        mesh=mesh,
        in_specs=placed,
        out_specs=(P("groups", "gx", "gy"), P("groups", "gy", "gx")),
        check_vma=False,
    )
```

profile of v0, /device:TPU:0, one launch (start us, length us, event | category | flops | bytes accessed | tf_op | source)
XLA Modules:
  0.0 342.2 jit_solution(1240028847422353079)
XLA Ops:
  8.4 3.8 %fusion.3 = f32[1,8,64,256]{3,2,1,0:T(8,128)S(1)} fusion(f32[64,256]{1,0:T(8,128)S(1)} %get-tuple-element.75, f32[64,256]{1,0:T(8,128)S(1)} %get-tuple-element.74, f32[64,256]{1,0:T(8,128)S(1)} %get-tuple-element.28, f32[64,256]{1,0:T(8,128)S(1)} %get-tuple-element.73, f32[64,256]{1,0:T(8,128)S(1)} %get-tuple-element.29, f32[8,64,256]{2,1,0:T(8,128)} %param.15, ...), kind=kLoop, calls=%fused_computation.31 | loop fusion | flops 1048576 | bytes 1441792 | tf_op jit(solution)/shard_map/stack | solution.py:141
  17.1 13.8 %all-gather = f32[1,128,128]{2,1,0:T(8,128)} all-gather(f32[1,32,128]{2,1,0:T(8,128)S(1)} %slice-done), channel_id=2, replica_groups=mesh['groups'=2,'gx'=4,'gy'=4] {'gx'}, dimensions={1}, use_global_device_ids=true | all-gather | bytes 81920 | tf_op jit(solution)/shard_map/all_gather | solution.py:135
  30.9 4.9 %all-to-all-start = ((f32[4,32,128]{2,1,0:T(8,128)}), f32[4,32,128]{2,1,0:T(8,128)S(1)}, u32[]{:S(2)}, u32[]{:S(2)}) async-start(f32[4,32,128]{2,1,0:T(8,128)} %bitcast.5), calls=%async_computation | async-start | bytes 131072 | tf_op jit(solution)/shard_map/all_to_all | solution.py:136
  36.8 3.9 %collective-permute-start.10 = (f32[2,8,1,258]{3,2,1,0:T(1,128)S(1)}, f32[2,8,1,258]{3,2,1,0:T(1,128)S(1)}, u32[]{:S(2)}, u32[]{:S(2)}) collective-permute-start(f32[2,8,1,258]{3,2,1,0:T(1,128)S(1)} %get-tuple-element.47), channel_id=1, source_target_pairs={{0,1},{1,2},{2,3},{4,5},{5,6},{6,7},{8,9},{9,10},{10,11},{12,13},{... | collective-permute-start | bytes 49544 | tf_op jit(solution)/shard_map/ppermute | solution.py:23
  42.3 4.2 %collective-permute-done.11 = f32[2,8,1,258]{3,2,1,0:T(1,128)S(1)} collective-permute-done((f32[2,8,1,258]{3,2,1,0:T(1,128)S(1)}, f32[2,8,1,258]{3,2,1,0:T(1,128)S(1)}, u32[]{:S(2)}, u32[]{:S(2)}) %collective-permute-start.11) | collective-permute-done | bytes 16544 | tf_op jit(solution)/shard_map/ppermute | solution.py:26
  47.3 3.4 fusion.16
  56.4 4.3 %collective-permute-start.1 = (f32[16,1,128]{2,1,0:T(1,128)}, f32[16,1,128]{2,1,0:T(1,128)}, u32[]{:S(2)}, u32[]{:S(2)}) collective-permute-start(f32[16,1,128]{2,1,0:T(1,128)} %get-tuple-element.71), channel_id=1, source_target_pairs={{0,4},{4,8},{8,12},{1,5},{5,9},{9,13},{2,6},{6,10},{10,14},{3,7},{... | collective-permute-start | bytes 24584 | tf_op jit(solution)/shard_map/ppermute | solution.py:23
  61.4 4.0 %collective-permute-start.14 = (f32[8,1,258]{2,1,0:T(1,128)}, f32[8,1,258]{2,1,0:T(1,128)}, u32[]{:S(2)}, u32[]{:S(2)}) collective-permute-start(f32[8,1,258]{2,1,0:T(1,128)} %get-tuple-element.56), channel_id=1, source_target_pairs={{0,1},{1,2},{2,3},{4,5},{5,6},{6,7},{8,9},{9,10},{10,11},{12,13},{... | collective-permute-start | bytes 24776 | tf_op jit(solution)/shard_map/ppermute | solution.py:23
  68.0 3.3 collective-permute-done.15
  72.7 4.9 %multiply_reduce_fusion.3 = (f32[]{:T(128)}, f32[]{:T(128)}, f32[8,64,256]{2,1,0:T(8,128)}) fusion(f32[8,64,256]{2,1,0:T(8,128)S(1)} %fusion.99, f32[8,64,256]{2,1,0:T(8,128)S(1)} %copy-done.11, f32[8,64,1]{2,1,0:T(8,128)S(1)} %collective-permute-done.12, f32[8,64,256]{2,1,0:T(8,128)S(1)} %copy-done.8, f32[8,64,1]{2,1,0:T(8,128)} %copy-done.20, ...), kind=kLoop, calls=%fused_computation.152 | loop fusion | flops 4718590 | bytes 5984392 | tf_op jit(solution)/shard_map/reduce_sum | solution.py:153
  77.6 31.2 %all-reduce.7 = (f32[]{:T(128)}, f32[]{:T(128)}) all-reduce(f32[]{:T(128)} %get-tuple-element.27, f32[]{:T(128)} %get-tuple-element.26), channel_id=1, replica_groups=mesh['groups'=2,'gx'=4,'gy'=4] {'gx','gy'}, use_global_device_ids=true, to_apply=%region_4.5 | all-reduce | flops 2 | bytes 16 | tf_op jit(solution)/shard_map/psum | solution.py:124
  112.0 31.7 %psum.44 = f32[]{:T(128)} all-reduce(f32[]{:T(128)} %get-tuple-element.35), channel_id=1, replica_groups=mesh['groups'=2,'gx'=4,'gy'=4] {'gx','gy'}, use_global_device_ids=true, to_apply=%region_8.9 | all-reduce | flops 1 | bytes 8 | tf_op jit(solution)/shard_map/psum | solution.py:124
  160.3 3.6 %multiply_reduce_fusion.1 = (f32[]{:T(128)}, f32[8,64,256]{2,1,0:T(8,128)}) fusion(f32[8,64,256]{2,1,0:T(8,128)S(1)} %multiply_add_fusion.1, f32[8,64,256]{2,1,0:T(8,128)S(1)} %copy-done.12, f32[8,64,1]{2,1,0:T(8,128)S(1)} %collective-permute-done.16, f32[8,64,256]{2,1,0:T(8,128)S(1)} %copy-done.9, f32[8,64,1]{2,1,0:T(8,128)S(1)} %collective-permute-done.17, ...), kind=kLoop, calls=%fused_computation.148 | loop fusion | flops 4456447 | bytes 5984388 | tf_op jit(solution)/shard_map/reduce_sum | solution.py:153
  163.9 32.3 %psum.45 = f32[]{:T(128)} all-reduce(f32[]{:T(128)} %get-tuple-element.33), channel_id=1, replica_groups=mesh['groups'=2,'gx'=4,'gy'=4] {'gx','gy'}, use_global_device_ids=true, to_apply=%region_10.11 | all-reduce | flops 1 | bytes 8 | tf_op jit(solution)/shard_map/psum | solution.py:153
  199.3 3.3 collective-permute-start.3
  202.6 34.1 %psum.46 = f32[]{:T(128)} all-reduce(f32[]{:T(128)} %multiply_reduce_fusion), channel_id=1, replica_groups=mesh['groups'=2,'gx'=4,'gy'=4] {'gx','gy'}, use_global_device_ids=true, to_apply=%region_12.13 | all-reduce | flops 1 | bytes 8 | tf_op jit(solution)/shard_map/psum | solution.py:124
  243.5 3.6 %collective-permute-done.21 = f32[8,64,1]{2,1,0:T(8,128)S(1)} collective-permute-done((f32[8,64,1]{2,1,0:T(8,128)S(1)}, f32[8,64,1]{2,1,0:T(8,128)S(1)}, u32[]{:S(2)}, u32[]{:S(2)}) %collective-permute-start.21) | collective-permute-done | bytes 2080 | tf_op jit(solution)/shard_map/ppermute | solution.py:26
  252.9 7.0 %collective-permute-start.5 = (f32[16,1,128]{2,1,0:T(1,128)S(1)}, f32[16,1,128]{2,1,0:T(1,128)S(1)}, u32[]{:S(2)}, u32[]{:S(2)}) collective-permute-start(f32[16,1,128]{2,1,0:T(1,128)S(1)} %get-tuple-element.69), channel_id=1, source_target_pairs={{0,4},{4,8},{8,12},{1,5},{5,9},{9,13},{2,6},{6,10},{10,14},{3,7},{... | collective-permute-start | bytes 24584 | tf_op jit(solution)/shard_map/ppermute | solution.py:23
  260.4 3.0 fusion.24
  263.5 32.7 %psum.47 = f32[]{:T(128)} all-reduce(f32[]{:T(128)} %fusion.24), channel_id=1, replica_groups=mesh['groups'=2,'gx'=4,'gy'=4] {'gx','gy'}, use_global_device_ids=true, to_apply=%region_14.15 | all-reduce | flops 1 | bytes 8 | tf_op jit(solution)/shard_map/psum | solution.py:153
  303.4 3.3 all-to-all-start.1
  308.2 4.6 %collective-permute-start.7 = (f32[16,34,1]{2,1,0:T(8,128)S(1)}, f32[16,34,1]{2,1,0:T(8,128)S(1)}, u32[]{:S(2)}, u32[]{:S(2)}) collective-permute-start(f32[16,34,1]{2,1,0:T(8,128)S(1)} %get-tuple-element.66), channel_id=1, source_target_pairs={{0,1},{1,2},{2,3},{4,5},{5,6},{6,7},{8,9},{9,10},{10,11},{12,13},{... | collective-permute-start | bytes 6536 | tf_op jit(solution)/shard_map/ppermute | solution.py:23
  313.5 3.7 %collective-permute-done.6 = f32[16,34,1]{2,1,0:T(8,128)S(1)} collective-permute-done((f32[16,34,1]{2,1,0:T(8,128)S(1)}, f32[16,34,1]{2,1,0:T(8,128)S(1)}, u32[]{:S(2)}, u32[]{:S(2)}) %collective-permute-start.6) | collective-permute-done | bytes 2208 | tf_op jit(solution)/shard_map/ppermute | solution.py:26
  318.2 15.7 %reduce-scatter.2.cloned.1.call-done = f32[32,128]{1,0:T(8,128)} async-done(((f32[128,128]{1,0:T(8,128)}), f32[32,128]{1,0:T(8,128)}) %reduce-scatter.2.cloned.1.call-update) | async-done | bytes 16400 | tf_op jit(solution)/shard_map/reduce_scatter | solution.py:164
  (171 shorter events, 60.3 us)
Async XLA Ops:
  13.4 23.2 %collective-permute-start.8 = (f32[2,8,64,1]{3,2,1,0:T(8,128)}, f32[2,8,64,1]{3,2,1,0:T(8,128)S(1)}, u32[]{:S(2)}, u32[]{:S(2)}) collective-permute-start(f32[2,8,64,1]{3,2,1,0:T(8,128)} %get-tuple-element.57), channel_id=1, source_target_pairs={{0,4},{4,8},{8,12},{1,5},{5,9},{9,13},{2,6},{6,10},{10,14},{3,7},{... | collective-permute-start | bytes 12296 | tf_op jit(solution)/shard_map/ppermute | solution.py:23
  15.8 20.8 %collective-permute-start.9 = (f32[2,8,64,1]{3,2,1,0:T(8,128)}, f32[2,8,64,1]{3,2,1,0:T(8,128)S(1)}, u32[]{:S(2)}, u32[]{:S(2)}) collective-permute-start(f32[2,8,64,1]{3,2,1,0:T(8,128)} %get-tuple-element.58), channel_id=1, source_target_pairs={{4,0},{8,4},{12,8},{5,1},{9,5},{13,9},{6,2},{10,6},{14,10},{7,3},{... | collective-permute-start | bytes 12296 | tf_op jit(solution)/shard_map/ppermute | solution.py:26
  30.9 19.8 %all-to-all-start = ((f32[4,32,128]{2,1,0:T(8,128)}), f32[4,32,128]{2,1,0:T(8,128)S(1)}, u32[]{:S(2)}, u32[]{:S(2)}) async-start(f32[4,32,128]{2,1,0:T(8,128)} %bitcast.5), calls=%async_computation | async-start | bytes 131072 | tf_op jit(solution)/shard_map/all_to_all | solution.py:136
  36.8 5.4 %collective-permute-start.10 = (f32[2,8,1,258]{3,2,1,0:T(1,128)S(1)}, f32[2,8,1,258]{3,2,1,0:T(1,128)S(1)}, u32[]{:S(2)}, u32[]{:S(2)}) collective-permute-start(f32[2,8,1,258]{3,2,1,0:T(1,128)S(1)} %get-tuple-element.47), channel_id=1, source_target_pairs={{0,1},{1,2},{2,3},{4,5},{5,6},{6,7},{8,9},{9,10},{10,11},{12,13},{... | collective-permute-start | bytes 49544 | tf_op jit(solution)/shard_map/ppermute | solution.py:23
  40.8 5.7 %collective-permute-start.11 = (f32[2,8,1,258]{3,2,1,0:T(1,128)S(1)}, f32[2,8,1,258]{3,2,1,0:T(1,128)S(1)}, u32[]{:S(2)}, u32[]{:S(2)}) collective-permute-start(f32[2,8,1,258]{3,2,1,0:T(1,128)S(1)} %get-tuple-element.48), channel_id=1, source_target_pairs={{1,0},{2,1},{3,2},{5,4},{6,5},{7,6},{9,8},{10,9},{11,10},{13,12},{... | collective-permute-start | bytes 49544 | tf_op jit(solution)/shard_map/ppermute | solution.py:26
  51.9 8.8 %collective-permute-start.12 = (f32[8,64,1]{2,1,0:T(8,128)S(1)}, f32[8,64,1]{2,1,0:T(8,128)S(1)}, u32[]{:S(2)}, u32[]{:S(2)}) collective-permute-start(f32[8,64,1]{2,1,0:T(8,128)S(1)} %get-tuple-element.64), channel_id=1, source_target_pairs={{0,4},{4,8},{8,12},{1,5},{5,9},{9,13},{2,6},{6,10},{10,14},{3,7},{... | collective-permute-start | bytes 6152 | tf_op jit(solution)/shard_map/ppermute | solution.py:23
  53.2 7.5 %collective-permute-start.13 = (f32[8,64,1]{2,1,0:T(8,128)S(1)}, f32[8,64,1]{2,1,0:T(8,128)S(1)}, u32[]{:S(2)}, u32[]{:S(2)}) collective-permute-start(f32[8,64,1]{2,1,0:T(8,128)S(1)} %get-tuple-element.63), channel_id=1, source_target_pairs={{4,0},{8,4},{12,8},{5,1},{9,5},{13,9},{6,2},{10,6},{14,10},{7,3},{... | collective-permute-start | bytes 6152 | tf_op jit(solution)/shard_map/ppermute | solution.py:26
  55.1 92.9 %collective-permute-start = (f32[16,1,128]{2,1,0:T(1,128)}, f32[16,1,128]{2,1,0:T(1,128)}, u32[]{:S(2)}, u32[]{:S(2)}) collective-permute-start(f32[16,1,128]{2,1,0:T(1,128)} %get-tuple-element.72), channel_id=1, source_target_pairs={{4,0},{8,4},{12,8},{5,1},{9,5},{13,9},{6,2},{10,6},{14,10},{7,3},{... | collective-permute-start | bytes 24584 | tf_op jit(solution)/shard_map/ppermute | solution.py:26
  56.4 91.7 %collective-permute-start.1 = (f32[16,1,128]{2,1,0:T(1,128)}, f32[16,1,128]{2,1,0:T(1,128)}, u32[]{:S(2)}, u32[]{:S(2)}) collective-permute-start(f32[16,1,128]{2,1,0:T(1,128)} %get-tuple-element.71), channel_id=1, source_target_pairs={{0,4},{4,8},{8,12},{1,5},{5,9},{9,13},{2,6},{6,10},{10,14},{3,7},{... | collective-permute-start | bytes 24584 | tf_op jit(solution)/shard_map/ppermute | solution.py:23
  61.4 6.6 %collective-permute-start.14 = (f32[8,1,258]{2,1,0:T(1,128)}, f32[8,1,258]{2,1,0:T(1,128)}, u32[]{:S(2)}, u32[]{:S(2)}) collective-permute-start(f32[8,1,258]{2,1,0:T(1,128)} %get-tuple-element.56), channel_id=1, source_target_pairs={{0,1},{1,2},{2,3},{4,5},{5,6},{6,7},{8,9},{9,10},{10,11},{12,13},{... | collective-permute-start | bytes 24776 | tf_op jit(solution)/shard_map/ppermute | solution.py:23
  65.4 6.0 %collective-permute-start.15 = (f32[8,1,258]{2,1,0:T(1,128)}, f32[8,1,258]{2,1,0:T(1,128)}, u32[]{:S(2)}, u32[]{:S(2)}) collective-permute-start(f32[8,1,258]{2,1,0:T(1,128)} %get-tuple-element.55), channel_id=1, source_target_pairs={{1,0},{2,1},{3,2},{5,4},{6,5},{7,6},{9,8},{10,9},{11,10},{13,12},{... | collective-permute-start | bytes 24776 | tf_op jit(solution)/shard_map/ppermute | solution.py:26
  151.4 6.6 %collective-permute-start.18 = (f32[8,1,258]{2,1,0:T(1,128)S(1)}, f32[8,1,258]{2,1,0:T(1,128)S(1)}, u32[]{:S(2)}, u32[]{:S(2)}) collective-permute-start(f32[8,1,258]{2,1,0:T(1,128)S(1)} %get-tuple-element.54), channel_id=1, source_target_pairs={{0,1},{1,2},{2,3},{4,5},{5,6},{6,7},{8,9},{9,10},{10,11},{12,13},{... | collective-permute-start | bytes 24776 | tf_op jit(solution)/shard_map/ppermute | solution.py:23
  154.3 5.6 %collective-permute-start.19 = (f32[8,1,258]{2,1,0:T(1,128)S(1)}, f32[8,1,258]{2,1,0:T(1,128)S(1)}, u32[]{:S(2)}, u32[]{:S(2)}) collective-permute-start(f32[8,1,258]{2,1,0:T(1,128)S(1)} %get-tuple-element.53), channel_id=1, source_target_pairs={{1,0},{2,1},{3,2},{5,4},{6,5},{7,6},{9,8},{10,9},{11,10},{13,12},{... | collective-permute-start | bytes 24776 | tf_op jit(solution)/shard_map/ppermute | solution.py:26
  156.5 85.5 %collective-permute-start.2 = (f32[16,34,1]{2,1,0:T(8,128)}, f32[16,34,1]{2,1,0:T(8,128)}, u32[]{:S(2)}, u32[]{:S(2)}) collective-permute-start(f32[16,34,1]{2,1,0:T(8,128)} %get-tuple-element.67), channel_id=1, source_target_pairs={{1,0},{2,1},{3,2},{5,4},{6,5},{7,6},{9,8},{10,9},{11,10},{13,12},{... | collective-permute-start | bytes 6536 | tf_op jit(solution)/shard_map/ppermute | solution.py:26
  199.3 42.6 %collective-permute-start.3 = (f32[16,34,1]{2,1,0:T(8,128)}, f32[16,34,1]{2,1,0:T(8,128)}, u32[]{:S(2)}, u32[]{:S(2)}) collective-permute-start(f32[16,34,1]{2,1,0:T(8,128)} %get-tuple-element.68), channel_id=1, source_target_pairs={{0,1},{1,2},{2,3},{4,5},{5,6},{6,7},{8,9},{9,10},{10,11},{12,13},{... | collective-permute-start | bytes 6536 | tf_op jit(solution)/shard_map/ppermute | solution.py:23
  240.7 6.5 %collective-permute-start.21 = (f32[8,64,1]{2,1,0:T(8,128)S(1)}, f32[8,64,1]{2,1,0:T(8,128)S(1)}, u32[]{:S(2)}, u32[]{:S(2)}) collective-permute-start(f32[8,64,1]{2,1,0:T(8,128)S(1)} %get-tuple-element.59), channel_id=1, source_target_pairs={{4,0},{8,4},{12,8},{5,1},{9,5},{13,9},{6,2},{10,6},{14,10},{7,3},{... | collective-permute-start | bytes 6152 | tf_op jit(solution)/shard_map/ppermute | solution.py:26
  247.3 12.6 %collective-permute-start.22 = (f32[8,1,258]{2,1,0:T(1,128)S(1)}, f32[8,1,258]{2,1,0:T(1,128)S(1)}, u32[]{:S(2)}, u32[]{:S(2)}) collective-permute-start(f32[8,1,258]{2,1,0:T(1,128)S(1)} %get-tuple-element.52), channel_id=1, source_target_pairs={{0,1},{1,2},{2,3},{4,5},{5,6},{6,7},{8,9},{9,10},{10,11},{12,13},{... | collective-permute-start | bytes 24776 | tf_op jit(solution)/shard_map/ppermute | solution.py:23
  250.1 9.8 %collective-permute-start.23 = (f32[8,1,258]{2,1,0:T(1,128)S(1)}, f32[8,1,258]{2,1,0:T(1,128)S(1)}, u32[]{:S(2)}, u32[]{:S(2)}) collective-permute-start(f32[8,1,258]{2,1,0:T(1,128)S(1)} %get-tuple-element.51), channel_id=1, source_target_pairs={{1,0},{2,1},{3,2},{5,4},{6,5},{7,6},{9,8},{10,9},{11,10},{13,12},{... | collective-permute-start | bytes 24776 | tf_op jit(solution)/shard_map/ppermute | solution.py:26
  251.6 11.8 %collective-permute-start.4 = (f32[16,1,128]{2,1,0:T(1,128)S(1)}, f32[16,1,128]{2,1,0:T(1,128)S(1)}, u32[]{:S(2)}, u32[]{:S(2)}) collective-permute-start(f32[16,1,128]{2,1,0:T(1,128)S(1)} %get-tuple-element.70), channel_id=1, source_target_pairs={{4,0},{8,4},{12,8},{5,1},{9,5},{13,9},{6,2},{10,6},{14,10},{7,3},{... | collective-permute-start | bytes 24584 | tf_op jit(solution)/shard_map/ppermute | solution.py:26
  252.9 10.5 %collective-permute-start.5 = (f32[16,1,128]{2,1,0:T(1,128)S(1)}, f32[16,1,128]{2,1,0:T(1,128)S(1)}, u32[]{:S(2)}, u32[]{:S(2)}) collective-permute-start(f32[16,1,128]{2,1,0:T(1,128)S(1)} %get-tuple-element.69), channel_id=1, source_target_pairs={{0,4},{4,8},{8,12},{1,5},{5,9},{9,13},{2,6},{6,10},{10,14},{3,7},{... | collective-permute-start | bytes 24584 | tf_op jit(solution)/shard_map/ppermute | solution.py:23
  303.4 9.4 %all-to-all-start.1 = ((f32[32,4,128]{2,0,1:T(8,128)}), f32[32,4,128]{2,0,1:T(8,128)S(1)}, u32[]{:S(2)}, u32[]{:S(2)}) async-start(f32[32,4,128]{2,0,1:T(8,128)} %copy.40), calls=%async_computation.1 | async-start | bytes 131072 | tf_op jit(solution)/shard_map/all_to_all | solution.py:163
  306.7 27.2 %reduce-scatter.2.cloned.1.call-start = ((), (), s32[]{:S(2)}) async-start(), calls=%async_computation.3 | async-start | bytes 81920 | tf_op jit(solution)/shard_map/reduce_scatter | solution.py:164
  306.9 10.2 %collective-permute-start.6 = (f32[16,34,1]{2,1,0:T(8,128)S(1)}, f32[16,34,1]{2,1,0:T(8,128)S(1)}, u32[]{:S(2)}, u32[]{:S(2)}) collective-permute-start(f32[16,34,1]{2,1,0:T(8,128)S(1)} %get-tuple-element.65), channel_id=1, source_target_pairs={{1,0},{2,1},{3,2},{5,4},{6,5},{7,6},{9,8},{10,9},{11,10},{13,12},{... | collective-permute-start | bytes 6536 | tf_op jit(solution)/shard_map/ppermute | solution.py:26
  308.2 9.5 %collective-permute-start.7 = (f32[16,34,1]{2,1,0:T(8,128)S(1)}, f32[16,34,1]{2,1,0:T(8,128)S(1)}, u32[]{:S(2)}, u32[]{:S(2)}) collective-permute-start(f32[16,34,1]{2,1,0:T(8,128)S(1)} %get-tuple-element.66), channel_id=1, source_target_pairs={{0,1},{1,2},{2,3},{4,5},{5,6},{6,7},{8,9},{9,10},{10,11},{12,13},{... | collective-permute-start | bytes 6536 | tf_op jit(solution)/shard_map/ppermute | solution.py:23
  (42 other events, 386.0 us)
Sparse Core Ops, SparseCore 0:
  313.6 20.2 reduce-scatter.1
where the time goes:
time: 344 us; the launch traced here: 342 us
  blocking collectives  176 us (51%)
  starting transfers between devices  63 us (18%)
  other arithmetic  36.5 us (11%)
  waiting for transfers between devices  35.6 us (10%)
  between operations  21.6 us (6%)
  local copies, waits for them, and re-layouts  7.95 us (2%)
    psum x3, blocking collectives, squares_sum(): return lax.psum(jnp.sum(vector * vector), ('gx', 'gy'))  97 us
    psum x2, blocking collectives, shards(): alpha_step = norm_now / lax.psum(jnp.sum(direction * image), ('gx', 'gy'))  65 us
    ppermute x12, starting transfers between devices, padded_2(): lax.ppermute(lax.slice_in_dim(block, block.shape[dim] - width, None, axis...  38.9 us
    ppermute x12, waiting for transfers between devices, padded_2(): lax.ppermute(lax.slice_in_dim(block, 0, width, axis=dim), axis, backward)  19.1 us
    ppermute x12, starting transfers between devices, padded_2(): lax.ppermute(lax.slice_in_dim(block, 0, width, axis=dim), axis, backward)  15.9 us
    reduce_scatter x1, waiting for transfers between devices, shards(): back = lax.psum_scatter(back_cols, 'gx', scatter_dimension=0, tiled=True)  15.7 us
    all_gather x1, blocking collectives, shards(): all_rows = lax.all_gather(theta[0], 'gx', axis=0, tiled=True)  13.8 us
    reduce_sum x3, other arithmetic, shards(): alpha_step = norm_now / lax.psum(jnp.sum(direction * image), ('gx', 'gy'))  11.5 us
  transfers between devices with their start and end apart: 27, of which 9 were waited for; matrix products, arithmetic and copies ran while one was open for 9% of the time, Pallas kernels for 0%

commit v1 on v0

v1 whole, which is shorter than its diff:
```python
import functools

import jax
import jax.numpy as jnp
from jax import lax
from jax.experimental import pallas as pl
from jax.experimental.pallas import tpu as pltpu
from jax.sharding import PartitionSpec as P

diffuse = 0.08
vertical_mix = 0.1
time_step = 4.0
infiltrate = 0.5
evaporate = 1.0
storage = 0.1

LANES = 128
SUB = 8
MESH = pl.DeviceIdType.MESH
HIGH = lax.Precision.HIGHEST
F32 = jnp.float32


def dot(a, b):
    return jnp.dot(a, b, precision=HIGH, preferred_element_type=F32)


def dot_nt(a, b):
    return lax.dot_general(
        a, b, (((1,), (1,)), ((), ())), precision=HIGH, preferred_element_type=F32
    )


def each(count, body):
    if count <= 16:
        for index in range(count):
            body(index)
    else:

        @pl.loop(0, count)
        def _(index):
            body(index)


def turn(value, amount, axis):
    size = value.shape[axis]
    amount = amount % size
    return value if amount == 0 else pltpu.roll(value, amount, axis)


def retention(head, alpha, expo):
    expo_m = 1.0 - 1.0 / expo
    power = expo * jnp.log(alpha * jnp.abs(head))
    log_u = jnp.log(1.0 + jnp.exp(power))
    return power, log_u, expo_m, jnp.exp(-0.25 * expo_m * log_u)


def pick(kind, table_ref):
    value = jnp.full(kind.shape, table_ref[0], F32)
    for index in range(1, table_ref.shape[0]):
        value = jnp.where(kind == float(index), table_ref[index], value)
    return value


def kernel(
    ngx,
    ngy,
    theta_hbm,
    terrain_hbm,
    head_hbm,
    soil_hbm,
    tiles_hbm,
    pair_ref,
    alpha_ref,
    expo_ref,
    ksat_ref,
    theta_out,
    head_out,
    th,
    sw,
    done,
    tr,
    hd,
    soil,
    soilf,
    tl,
    rowh,
    rows_soil,
    pack,
    colr,
    corner,
    gath,
    trs,
    trr,
    tcs,
    tcr,
    root,
    cap,
    diag,
    vec0,
    vec1,
    vec2,
    wvec,
    mom,
    momr,
    bsend,
    brecv,
    local_sem,
    out_sem,
    near_send,
    near_recv,
    g_send,
    g_recv,
    t_send,
    t_recv,
    m_send,
    m_recv,
    b_send,
    b_recv,
):
    x = lax.axis_index("gx")
    y = lax.axis_index("gy")
    levs, height, width = head_hbm.shape
    lev, th_rows, _ = theta_hbm.shape
    tile_count = width // LANES
    nblock = gath.shape[0]
    ratio = height // 2 // th_rows
    group = ngx * ngy
    me = x * ngy + y
    ext_h, ext_w = height + SUB, width + LANES
    low, high_x = x > 0, x < ngx - 1
    left, right_y = y > 0, y < ngy - 1

    loads = []

    def load(src, dst):
        copy = pltpu.make_async_copy(src, dst, local_sem.at[len(loads)])
        copy.start()
        loads.append(copy)
        return copy

    c_theta = load(theta_hbm, th)
    c_head = load(head_hbm, hd.at[:, 0:height, 0:width])
    c_soil = load(soil_hbm, soil)
    c_terrain = load(terrain_hbm, tr)
    first = x * tile_count
    total_tiles = tiles_hbm.shape[0]
    tile_at = [
        jnp.minimum(jnp.maximum(first + i - 1, 0), total_tiles - 1)
        for i in range(tile_count + 2)
    ]
    c_tiles = [load(tiles_hbm.at[tile_at[i]], tl.at[i]) for i in range(tile_count + 2)]

    rowh[...] = jnp.zeros(rowh.shape, F32)
    rows_soil[...] = jnp.zeros(rows_soil.shape, jnp.int32)
    colr[...] = jnp.zeros(colr.shape, F32)
    corner[...] = jnp.zeros(corner.shape, F32)
    gath[...] = jnp.zeros(gath.shape, F32)
    trr[...] = jnp.zeros(trr.shape, F32)
    tcr[...] = jnp.zeros(tcr.shape, F32)

    barrier = pltpu.get_barrier_semaphore()

    def greet(index):
        @pl.when(index != me)
        def _():
            pl.semaphore_signal(
                barrier,
                inc=1,
                device_id={"gx": index // ngy, "gy": index % ngy},
                device_id_type=MESH,
            )

    each(group, greet)

    lane = lax.broadcasted_iota(jnp.int32, (1, LANES), 1)

    def pack_theta(sweep, source):
        trs[sweep, 0] = source[:, 0, :]
        trs[sweep, 1] = source[:, th_rows - 1, :]
        first_col = jnp.zeros((th_rows, LANES), F32)
        last_col = jnp.zeros((th_rows, LANES), F32)
        for k in range(lev):
            first_col = jnp.where(lane == k, turn(source[k], k, 1), first_col)
            last_col = jnp.where(lane == k, turn(source[k], k + 1, 1), last_col)
        tcs[sweep, 0] = first_col
        tcs[sweep, 1] = last_col

    c_theta.wait()
    pack_theta(0, th)

    c_head.wait()
    c_soil.wait()
    soilf[0:height, 0:width] = soil[...].astype(F32)
    edge_l = jnp.zeros((height, LANES), F32)
    edge_r = jnp.zeros((height, LANES), F32)
    for k in range(levs + 1):
        if k < levs:
            a, b = hd[k, 0:height, 0:LANES], hd[k, 0:height, width - LANES : width]
        else:
            a, b = soilf[0:height, 0:LANES], soilf[0:height, width - LANES : width]
        edge_l = jnp.where(lane // 4 == k, turn(a, 4 * k, 1), edge_l)
        edge_r = jnp.where((LANES - 1 - lane) // 4 == k, turn(b, -4 * k, 1), edge_r)
    pack[0] = edge_l
    pack[1] = edge_r

    pl.semaphore_wait(barrier, group - 1)

    sent = []

    def remote(src, dst, ssem, rsem, to):
        return pltpu.make_async_remote_copy(
            src_ref=src,
            dst_ref=dst,
            send_sem=ssem,
            recv_sem=rsem,
            device_id={"gx": to[0], "gy": to[1]},
            device_id_type=MESH,
        )

    def send(cond, *what):
        @pl.when(cond)
        def _():
            remote(*what).start()

        sent.append((cond, what))

    def arrive(cond, dst, rsem):
        @pl.when(cond)
        def _():
            remote(dst, dst, near_send.at[0], rsem, (x, y)).wait_recv()

    near = []

    def halo(index, cond, src, dst, to, cond_in):
        send(cond, src, dst, near_send.at[index], near_recv.at[index], to)
        near.append((cond_in, dst, near_recv.at[index]))

    halo(0, left, head_hbm.at[:, 0:SUB, :], rowh.at[0], (x, y - 1), right_y)
    halo(1, right_y, head_hbm.at[:, height - SUB :, :], rowh.at[1], (x, y + 1), left)
    halo(2, low, pack.at[0], colr.at[0], (x - 1, y), high_x)
    halo(3, high_x, pack.at[1], colr.at[1], (x + 1, y), low)

    dest = x // ratio
    part = x % ratio
    offset = pl.multiple_of(part * th_rows, th_rows)
    body = ratio * th_rows

    def spread(kind, cond, dest_y, src, dst, slot):
        def one(i):
            me_too = jnp.logical_and(i == x, dest_y == y)

            @pl.when(jnp.logical_and(cond, jnp.logical_not(me_too)))
            def _():
                remote(
                    src, dst, g_send.at[kind, i], g_recv.at[kind, slot], (i, dest_y)
                ).start()

        each(ngx, one)

        @pl.when(jnp.logical_and(cond, dest_y == y))
        def _():
            dst[...] = src[...]

        def finish(i):
            me_too = jnp.logical_and(i == x, dest_y == y)

            @pl.when(jnp.logical_and(cond, jnp.logical_not(me_too)))
            def _():
                remote(
                    src, dst, g_send.at[kind, i], g_recv.at[kind, slot], (i, dest_y)
                ).wait_send()

        return lambda: each(ngx, finish)

    slot = y * ratio + part
    at_first, at_last = part == 0, part == ratio - 1
    finish_spread = [
        spread(0, x >= 0, dest, th.at[0], gath.at[y, pl.ds(offset, th_rows)], slot),
        spread(
            1,
            jnp.logical_and(at_first, dest > 0),
            dest - 1,
            th.at[0, 0:SUB],
            gath.at[y, body : body + SUB],
            y,
        ),
        spread(
            2,
            jnp.logical_and(at_last, dest < ngy - 1),
            dest + 1,
            th.at[0, th_rows - SUB : th_rows],
            gath.at[y, body + SUB : body + 2 * SUB],
            y,
        ),
    ]

    halo(4, left, soil_hbm.at[0:SUB, :], rows_soil.at[0], (x, y - 1), right_y)
    halo(5, right_y, soil_hbm.at[height - SUB :, :], rows_soil.at[1], (x, y + 1), left)
    both = jnp.logical_and
    halo(6, both(low, left), pack.at[0, 0:SUB], corner.at[0], (x - 1, y - 1), both(high_x, right_y))
    halo(7, both(low, right_y), pack.at[0, height - SUB :], corner.at[1], (x - 1, y + 1), both(high_x, left))
    halo(8, both(high_x, left), pack.at[1, 0:SUB], corner.at[2], (x + 1, y - 1), both(low, right_y))
    halo(9, both(high_x, right_y), pack.at[1, height - SUB :], corner.at[3], (x + 1, y + 1), both(low, left))

    theta_in = []

    def theta_halo(sweep):
        got = []
        plan = (
            (low, trs, trr, 0, (x - 1, y), high_x),
            (high_x, trs, trr, 1, (x + 1, y), low),
            (left, tcs, tcr, 0, (x, y - 1), right_y),
            (right_y, tcs, tcr, 1, (x, y + 1), left),
        )
        for index, (cond, src, dst, side, to, cond_in) in enumerate(plan):
            send(
                cond,
                src.at[sweep, side],
                dst.at[sweep, side],
                t_send.at[sweep, index],
                t_recv.at[sweep, index],
                to,
            )
            got.append((cond_in, dst.at[sweep, side], t_recv.at[sweep, index]))
        theta_in.append(got)

    theta_halo(0)

    def state(k, rows, cols, alpha, expo, kmax, mask):
        power, log_u, expo_m, quarter = retention(hd[k, rows, cols], alpha, expo)
        sat = (quarter * quarter) * (quarter * quarter)
        cap[k, rows, cols] = (storage + sat) * (1.0 / time_step)
        value = jnp.sqrt(kmax) * quarter * (1.0 - jnp.exp(expo_m * (power - log_u)))
        root[k, rows, cols] = value if mask is None else jnp.where(mask, value, 0.0)

    def state_block(rows, cols, mask):
        kind = soilf[rows, cols]
        alpha, expo, kmax = (
            pick(kind, alpha_ref),
            pick(kind, expo_ref),
            pick(kind, ksat_ref),
        )
        for k in range(levs):
            state(k, rows, cols, alpha, expo, kmax, mask)

    for row in range(0, height, 32):
        state_block(slice(row, row + 32), slice(0, width), None)

    def sweep_once(sweep, source, store):
        for cond, dst, sem in theta_in[sweep]:
            arrive(cond, dst, sem)
        row_at = lax.broadcasted_iota(jnp.int32, (th_rows, LANES), 0)
        metric = diffuse * tr[...]
        from_right, from_left = tcr[sweep, 0], tcr[sweep, 1]
        for k in range(lev):
            centre = source[k]
            down = jnp.where(
                row_at == th_rows - 1, trr[sweep, 0, k : k + 1, :], turn(centre, -1, 0)
            )
            up = jnp.where(row_at == 0, trr[sweep, 1, k : k + 1, :], turn(centre, 1, 0))
            east = jnp.where(
                lane == LANES - 1, turn(from_right, LANES - 1 - k, 1), turn(centre, -1, 1)
            )
            west = jnp.where(lane == 0, turn(from_left, -k, 1), turn(centre, 1, 1))
            flat = down + up + east + west - 4.0 * centre
            vert = -2.0 * centre
            if k > 0:
                vert = vert + source[k - 1]
            if k < lev - 1:
                vert = vert + source[k + 1]
            store(k, centre + metric * flat + vertical_mix * vert)

    def store_first(k, value):
        sw[k] = value

    c_terrain.wait()
    sweep_once(0, th, store_first)
    pack_theta(1, sw)
    theta_halo(1)

    for cond, dst, sem in near:
        arrive(cond, dst, sem)
    upper = lax.broadcasted_iota(jnp.int32, (SUB, 1), 0) < 4
    first_half = lane < LANES // 2
    for k in range(levs):
        hd[k, height:ext_h, 0:width] = jnp.where(upper, rowh[0, k], rowh[1, k])
    soilf[height:ext_h, 0:width] = jnp.where(upper, rows_soil[0], rows_soil[1]).astype(F32)
    right_side, left_side = colr[0], colr[1]
    right_corner = jnp.where(upper, corner[0], corner[1])
    left_corner = jnp.where(upper, corner[2], corner[3])
    for k in range(levs + 1):
        side = jnp.where(first_half, turn(right_side, -4 * k, 1), turn(left_side, 4 * k, 1))
        tip = jnp.where(first_half, turn(right_corner, -4 * k, 1), turn(left_corner, 4 * k, 1))
        if k < levs:
            hd[k, 0:height, width:ext_w] = side
            hd[k, height:ext_h, width:ext_w] = tip
        else:
            soilf[0:height, width:ext_w] = side
            soilf[height:ext_h, width:ext_w] = tip

    col_ok = jnp.logical_or(
        jnp.logical_and(lane < 4, high_x), jnp.logical_and(lane >= LANES - 4, low)
    )
    row_ok = jnp.logical_or(
        jnp.logical_and(upper, right_y), jnp.logical_and(jnp.logical_not(upper), left)
    )
    state_block(
        slice(0, height), slice(width, ext_w), jnp.broadcast_to(col_ok, (height, LANES))
    )
    state_block(
        slice(height, ext_h), slice(0, width), jnp.broadcast_to(row_ok, (SUB, width))
    )
    state_block(
        slice(height, ext_h), slice(width, ext_w), jnp.logical_and(row_ok, col_ok)
    )

    def arrive_blocks(kind, cond, from_x, dst_of, slot_of):
        def one(b):
            mine = jnp.logical_and(from_x == x, b == y)

            @pl.when(jnp.logical_and(cond, jnp.logical_not(mine)))
            def _():
                dst = dst_of(b)
                remote(dst, dst, near_send.at[0], g_recv.at[kind, slot_of(b)], (x, y)).wait_recv()

        each(nblock, one)

    for r in range(ratio):
        arrive_blocks(
            0,
            x >= 0,
            y * ratio + r,
            lambda b, r=r: gath.at[b, r * th_rows : (r + 1) * th_rows],
            lambda b, r=r: b * ratio + r,
        )
    arrive_blocks(
        1, right_y, (y + 1) * ratio, lambda b: gath.at[b, body : body + SUB], lambda b: b
    )
    arrive_blocks(
        2,
        left,
        y * ratio - 1,
        lambda b: gath.at[b, body + SUB : body + 2 * SUB],
        lambda b: b,
    )
    for copy in c_tiles:
        copy.wait()
    grow_to = lax.broadcasted_iota(jnp.int32, (ext_h, body + 2 * SUB), 0)
    grow_from = lax.broadcasted_iota(jnp.int32, (ext_h, body + 2 * SUB), 1)
    source_row = jnp.where(
        grow_to < height + 4, grow_to // 2, body + 2 * SUB - 2 + (grow_to - height - 4) // 2
    )
    grow = jnp.where(grow_from == source_row, infiltrate, 0.0).astype(F32)

    def down(i):
        total = None
        for q in range(2):
            term = dot(gath[pair_ref[tile_at[i], q]], tl[i, q])
            total = term if total is None else total + term
        return total

    infil = [dot(grow, down(i + 1)) for i in range(tile_count)]
    ends = jnp.where(first_half, down(tile_count + 1), down(0))
    infil.append(dot(grow, ends))

    def across(value):
        return (turn(value, 1, 1) + turn(value, -1, 1)) + (
            turn(value, 1, 0) + turn(value, -1, 0)
        )

    def around(ref, k):
        total = across(ref[k])
        if k > 0:
            total = total + ref[k - 1]
        if k < levs - 1:
            total = total + ref[k + 1]
        return total

    for k in range(levs):
        wvec[0, k] = root[k] * hd[k]
    for k in range(levs):
        centre = root[k]
        span = around(root, k)
        flow = around(wvec.at[0], k) - span * hd[k]
        if k > 0:
            flow = flow - root[k - 1]
        if k < levs - 1:
            flow = flow + root[k + 1]
        rhs = centre * flow
        if k == 0:
            rhs = rhs + jnp.concatenate(infil, axis=1)
        diag[k] = cap[k] + centre * span
        vec0[k] = rhs
        wvec[1, k] = centre * rhs

    def fold(value):
        part = None
        for c in range(0, width, LANES):
            for r in range(0, height, SUB):
                piece = value[r : r + SUB, c : c + LANES]
                part = piece if part is None else part + piece
        return part

    def plus(total, value):
        return value if total is None else total + value

    sums = [None] * 6
    for k in range(levs):
        here = vec0[k]
        image = diag[k] * here - root[k] * around(wvec.at[1], k)
        vec1[k] = image
        wvec[0, k] = root[k] * image
        sums[0] = plus(sums[0], fold(here * here))
        sums[1] = plus(sums[1], fold(here * image))
        sums[2] = plus(sums[2], fold(image * image))
    for k in range(levs):
        here = vec1[k]
        image = diag[k] * here - root[k] * around(wvec.at[0], k)
        vec2[k] = image
        wvec[1, k] = root[k] * image
        sums[3] = plus(sums[3], fold(here * image))
        sums[4] = plus(sums[4], fold(image * image))
    for k in range(levs):
        here = vec2[k]
        image = diag[k] * here - root[k] * around(wvec.at[1], k)
        sums[5] = plus(sums[5], fold(here * image))

    row8 = lax.broadcasted_iota(jnp.int32, (SUB, LANES), 0)
    packed = jnp.zeros((SUB, LANES), F32)
    for index, value in enumerate(sums):
        packed = jnp.where(row8 == index, jnp.sum(value, axis=0, keepdims=True), packed)
    mom[...] = packed
    momr[me] = packed

    def tell(index):
        @pl.when(index != me)
        def _():
            remote(
                mom, momr.at[me], m_send.at[index], m_recv.at[me], (index // ngy, index % ngy)
            ).start()

    each(group, tell)

    def store_second(k, value):
        done[k] = value

    sweep_once(1, sw, store_second)
    out_theta = pltpu.make_async_copy(done.at[1:lev], theta_out.at[1:lev], out_sem.at[0])
    out_theta.start()

    def hear(index):
        @pl.when(index != me)
        def _():
            remote(mom, momr.at[index], near_send.at[0], m_recv.at[index], (x, y)).wait_recv()

    each(group, hear)
    moments = jnp.sum(jnp.sum(momr[...], axis=0), axis=1, keepdims=True)
    mu = [moments[i : i + 1, :] for i in range(6)]
    scale = mu[1] / mu[0]
    inverse = mu[0] / mu[1]
    nu = []
    factor = 1.0 / mu[0]
    for i in range(6):
        nu.append(mu[i] * factor)
        factor = factor * inverse
    tiny = 1e-7
    l1, l2 = nu[2] / nu[1], nu[3] / nu[1]
    a11 = jnp.maximum(nu[3] - l1 * nu[2], tiny * nu[3])
    a12 = nu[4] - l1 * nu[3]
    b1 = nu[1] - l1 * nu[0]
    ratio_l = a12 / a11
    a22 = jnp.maximum(nu[5] - l2 * nu[3] - ratio_l * a12, tiny * nu[5])
    b2 = nu[2] - l2 * nu[0] - ratio_l * b1
    c2 = b2 / a22
    c1 = (b1 - a12 * c2) / a11
    c0 = (nu[0] - nu[2] * c1 - nu[3] * c2) / nu[1]
    c0 = c0 * inverse
    c1 = c1 * inverse * inverse
    c2 = c2 * inverse * inverse * inverse

    def advance_head(k):
        own = (k, slice(0, height), slice(0, width))
        value = hd[own] + (c0 * vec0[own] + c1 * vec1[own] + c2 * vec2[own])
        hd[own] = value
        return value

    surface = advance_head(0)
    kind = soilf[0:height, 0:width]
    _, _, _, quarter = retention(surface, pick(kind, alpha_ref), pick(kind, expo_ref))
    moist = (quarter * quarter) * (quarter * quarter)
    pair_row = lax.broadcasted_iota(jnp.int32, (body, height), 0)
    pair_col = lax.broadcasted_iota(jnp.int32, (body, height), 1)
    halver = jnp.where(pair_col // 2 == pair_row, 0.5, 0.0).astype(F32)
    halves = dot(halver, moist)
    contrib = []
    for i in range(tile_count):
        for q in range(2):
            contrib.append(
                (
                    pair_ref[first + i, q],
                    dot_nt(halves[:, i * LANES : (i + 1) * LANES], tl[i + 1, q]),
                )
            )

    for t in range(nblock):
        total = jnp.zeros((body, LANES), F32)
        for where_to, value in contrib:
            total = total + jnp.where(where_to == t, value, 0.0)
        for r in range(ratio):
            piece = total[r * th_rows : (r + 1) * th_rows]
            bsend[t * ratio + r] = piece
            to_x = y * ratio + r
            mine = jnp.logical_and(to_x == x, y == t)

            @pl.when(mine)
            def _():
                brecv[x] = piece

            @pl.when(jnp.logical_not(mine))
            def _():
                remote(
                    bsend.at[t * ratio + r],
                    brecv.at[x],
                    b_send.at[t * ratio + r],
                    b_recv.at[x],
                    (to_x, t),
                ).start()

    for k in range(1, levs):
        advance_head(k)
    out_head = pltpu.make_async_copy(
        hd.at[:, 0:height, 0:width], head_out, out_sem.at[1]
    )
    out_head.start()

    own_y = x // ratio

    def collect(index):
        mine = jnp.logical_and(index == x, own_y == y)

        @pl.when(jnp.logical_not(mine))
        def _():
            remote(
                brecv.at[index], brecv.at[index], near_send.at[0], b_recv.at[index], (x, y)
            ).wait_recv()

    each(ngx, collect)
    done[0] = done[0] + evaporate * jnp.sum(brecv[...], axis=0)
    out_level = pltpu.make_async_copy(done.at[0], theta_out.at[0], out_sem.at[2])
    out_level.start()

    for cond, what in sent:

        @pl.when(cond)
        def _():
            remote(*what).wait_send()

    for finish in finish_spread:
        finish()

    def told(index):
        @pl.when(index != me)
        def _():
            remote(
                mom, momr.at[me], m_send.at[index], m_recv.at[me], (index // ngy, index % ngy)
            ).wait_send()

    each(group, told)
    for t in range(nblock):
        for r in range(ratio):
            to_x = y * ratio + r

            @pl.when(jnp.logical_not(jnp.logical_and(to_x == x, y == t)))
            def _():
                remote(
                    bsend.at[t * ratio + r],
                    brecv.at[x],
                    b_send.at[t * ratio + r],
                    b_recv.at[x],
                    (to_x, t),
                ).wait_send()

    out_theta.wait()
    out_head.wait()
    out_level.wait()


def shards(ngx, ngy, theta, terrain, head, soil, pair_map, tiles, vg_alpha, vg_n, ksat):
    lev, th_rows, _ = theta.shape
    levs, height, width = head.shape
    body = height // 2
    ratio = body // th_rows
    tile_count = width // LANES
    ext = (levs, height + SUB, width + LANES)
    dma = pltpu.SemaphoreType.DMA
    group = ngx * ngy
    anywhere = pl.BlockSpec(memory_space=pl.ANY)
    scalars = pl.BlockSpec(memory_space=pltpu.SMEM)
    vmem = lambda *shape: pltpu.VMEM(shape, F32)
    return pl.pallas_call(
        functools.partial(kernel, ngx, ngy),
        out_shape=(
            jax.ShapeDtypeStruct(theta.shape, F32),
            jax.ShapeDtypeStruct(head.shape, F32),
        ),
        in_specs=[anywhere] * 5 + [scalars] * 4,
        out_specs=(anywhere, anywhere),
        scratch_shapes=[
            vmem(*theta.shape),
            vmem(*theta.shape),
            vmem(*theta.shape),
            vmem(*terrain.shape),
            vmem(*ext),
            pltpu.VMEM((height, width), jnp.int32),
            vmem(*ext[1:]),
            vmem(tile_count + 2, 2, LANES, LANES),
            vmem(2, levs, SUB, width),
            pltpu.VMEM((2, SUB, width), jnp.int32),
            vmem(2, height, LANES),
            vmem(2, height, LANES),
            vmem(4, SUB, LANES),
            vmem(ngy, body + 2 * SUB, LANES),
            vmem(2, 2, lev, LANES),
            vmem(2, 2, lev, LANES),
            vmem(2, 2, th_rows, LANES),
            vmem(2, 2, th_rows, LANES),
            vmem(*ext),
            vmem(*ext),
            vmem(*ext),
            vmem(*ext),
            vmem(*ext),
            vmem(*ext),
            vmem(2, *ext),
            vmem(SUB, LANES),
            vmem(group, SUB, LANES),
            vmem(ngy * ratio, th_rows, LANES),
            vmem(ngx, th_rows, LANES),
            dma((tile_count + 6,)),
            dma((3,)),
            dma((10,)),
            dma((10,)),
            dma((3, ngx)),
            dma((3, ngy * ratio)),
            dma((2, 4)),
            dma((2, 4)),
            dma((group,)),
            dma((group,)),
            dma((ngy * ratio,)),
            dma((ngx,)),
        ],
        compiler_params=pltpu.CompilerParams(
            collective_id=0, has_side_effects=True, vmem_limit_bytes=40 * 1024 * 1024
        ),
        name="coupled_step",
    )(theta, terrain, head, soil, tiles, pair_map, vg_alpha, vg_n, ksat)


def solution(mesh):
    placed = (
        P("groups", "gx", "gy"),
        P(("groups", "gx"), "gy"),
        P("groups", "gy", "gx"),
        P(("groups", "gy"), "gx"),
        P(),
        P(),
        P(),
        P(),
        P(),
    )
    return jax.shard_map(
        functools.partial(shards, mesh.shape["gx"], mesh.shape["gy"]),
        mesh=mesh,
        in_specs=placed,
        out_specs=(P("groups", "gx", "gy"), P("groups", "gy", "gx")),
        check_vma=False,
    )
```

time: 344 us -> 35.1 us (0.10)
  blocking collectives: 176 us -> 0 us
  starting transfers between devices: 63 us -> 0 us
  other arithmetic: 36.5 us -> 0 us
  waiting for transfers between devices: 35.6 us -> 0 us
  Pallas kernels: 0 us -> 27 us
  between operations: 21.6 us -> 0.68 us
    psum x5 -> x0, blocking collectives: 162 us -> none  [the longest x3 97 us: squares_sum(): return lax.psum(jnp.sum(vector * vector), ('gx', 'gy'))]
    ppermute x24 -> x0, starting transfers between devices: 54.9 us -> none  [the longest x12 38.9 us: padded_2(): lax.ppermute(lax.slice_in_dim(block, block.shape[dim] - width, None, axis...]
    pallas_call x0 -> x1, Pallas kernels: none -> 27 us  [shards(): pl.pallas_call(functools.partial(kernel, ngx, ngy), out_shape=(jax.ShapeD...]
    ppermute x24 -> x0, waiting for transfers between devices: 19.9 us -> none  [the longest x12 19.1 us: padded_2(): lax.ppermute(lax.slice_in_dim(block, 0, width, axis=dim), axis, backward)]
    reduce_sum x6 -> x0, other arithmetic: 16.3 us -> none  [the longest x3 11.5 us: shards(): alpha_step = norm_now / lax.psum(jnp.sum(direction * image), ('gx', 'gy'))]
    reduce_scatter x1 -> x0, waiting for transfers between devices: 15.7 us -> none  [shards(): back = lax.psum_scatter(back_cols, 'gx', scatter_dimension=0, tiled=True)]
    all_gather x1 -> x0, blocking collectives: 13.8 us -> none  [shards(): all_rows = lax.all_gather(theta[0], 'gx', axis=0, tiled=True)]
    all_to_all x2 -> x0, starting transfers between devices: 8.15 us -> none  [the longest x1 4.87 us: shards(): lax.all_to_all(all_rows, 'gy', split_axis=0, concat_axis=1, tiled=True)]
  transfers between devices with their start and end apart: 27 -> 0, of which waited for: 9 -> 0; matrix products, arithmetic and copies ran while one was open for 9% -> 0% of each run, Pallas kernels for 0% -> 0%
where the time goes in v1:
time: 35.1 us; the launch traced here: 34.7 us
  Pallas kernels  27 us (77%)
  local copies, waits for them, and re-layouts  7.05 us (20%)
  between operations  0.68 us (2%)
    pallas_call x1, Pallas kernels, shards(): pl.pallas_call(functools.partial(kernel, ngx, ngy), out_shape=(jax.ShapeD...  27 us
    unnamed x19, local copies, waits for them, and re-layouts  7.05 us

profile of v1, /device:TPU:0, one launch (start us, length us, event | category | flops | bytes accessed | tf_op | source)
XLA Modules:
  0.0 34.7 jit_solution(12358555388982144720)
XLA Ops:
  0.6 0.0 copy-start.7
  0.6 0.0 copy-start.6
  0.7 0.0 copy-start.5
  0.7 0.8 %copy.11.pair_ref = s32[8,2]{1,0:T(8,128)S(1)} copy(s32[8,2]{0,1:T(2,128)} %param.13) | data formatting | bytes 128 | tf_op args[4]
  1.4 0.0 copy-done.7
  1.4 0.0 copy-done.6
  1.4 0.0 copy-done.5
  1.4 0.0 copy-start
  1.4 1.2 %copy-done = f32[8,2,128,128]{3,2,1,0:T(8,128)S(1)} copy-done((f32[8,2,128,128]{3,2,1,0:T(8,128)S(1)}, f32[8,2,128,128]{3,2,1,0:T(8,128)}, u32[]{:S(2)}) %copy-start) | copy-done | bytes 1048600
  2.7 0.0 copy-start.1
  2.7 1.0 %copy-done.1 = f32[8,64,256]{2,1,0:T(8,128)S(1)} copy-done((f32[8,64,256]{2,1,0:T(8,128)S(1)}, f32[8,64,256]{2,1,0:T(8,128)}, u32[]{:S(2)}) %copy-start.1) | copy-done | bytes 524312
  3.7 0.0 copy-start.2
  3.7 0.9 %copy-done.2 = f32[16,32,128]{2,1,0:T(8,128)S(1)} copy-done((f32[16,32,128]{2,1,0:T(8,128)S(1)}, f32[16,32,128]{2,1,0:T(8,128)}, u32[]{:S(2)}) %copy-start.2) | copy-done | bytes 262168
  4.7 0.0 copy-start.3
  4.7 0.8 %copy-done.3 = s32[64,256]{1,0:T(8,128)S(1)} copy-done((s32[64,256]{1,0:T(8,128)S(1)}, s32[64,256]{1,0:T(8,128)}, u32[]{:S(2)}) %copy-start.3) | copy-done | bytes 65560
  5.5 0.0 copy-start.4
  5.5 0.7 %copy-done.4 = f32[32,128]{1,0:T(8,128)S(1)} copy-done((f32[32,128]{1,0:T(8,128)S(1)}, f32[32,128]{1,0:T(8,128)}, u32[]{:S(2)}) %copy-start.4) | copy-done | bytes 16408
  6.2 27.0 %coupled_step.1 = (f32[16,32,128]{2,1,0:T(8,128)S(1)}, f32[8,64,256]{2,1,0:T(8,128)S(1)}) custom-call(f32[16,32,128]{2,1,0:T(8,128)S(1)} %copy-done.2, f32[32,128]{1,0:T(8,128)S(1)} %copy-done.4, f32[8,64,256]{2,1,0:T(8,128)S(1)} %copy-done.1, s32[64,256]{1,0:T(8,128)S(1)} %copy-done.3, f32[8,2,128,128]{3,2,1,0:T(8,128)S(1)} %copy-done, ...), custom_call_target="tpu_custom_call" | custom-call | tf_op jit(solution)/shard_map/coupled_step/pallas_call | solution.py:701
  33.2 0.7 %copy.14 = f32[16,32,128]{2,1,0:T(8,128)} copy(f32[16,32,128]{2,1,0:T(8,128)S(1)} %get-tuple-element.4) | data formatting | bytes 524288
  34.0 0.8 %copy.15 = f32[8,64,256]{2,1,0:T(8,128)} copy(f32[8,64,256]{2,1,0:T(8,128)S(1)} %get-tuple-element.5) | data formatting | bytes 1048576
Async XLA Ops:
  0.6 0.8 %copy-start.7 = (f32[8]{0:T(128)S(1)}, f32[8]{0:T(128)}, u32[]{:S(2)}) copy-start(f32[8]{0:T(128)} %ksat_ref.1) | copy-start | bytes 100
  0.6 0.8 %copy-start.6 = (f32[8]{0:T(128)S(1)}, f32[8]{0:T(128)}, u32[]{:S(2)}) copy-start(f32[8]{0:T(128)} %expo_ref.1) | copy-start | bytes 100
  0.7 0.8 %copy-start.5 = (f32[8]{0:T(128)S(1)}, f32[8]{0:T(128)}, u32[]{:S(2)}) copy-start(f32[8]{0:T(128)} %alpha_ref.1) | copy-start | bytes 100
  1.4 1.2 %copy-start = (f32[8,2,128,128]{3,2,1,0:T(8,128)S(1)}, f32[8,2,128,128]{3,2,1,0:T(8,128)}, u32[]{:S(2)}) copy-start(f32[8,2,128,128]{3,2,1,0:T(8,128)} %tiles_hbm.1) | copy-start | bytes 3145732
  2.7 1.0 %copy-start.1 = (f32[8,64,256]{2,1,0:T(8,128)S(1)}, f32[8,64,256]{2,1,0:T(8,128)}, u32[]{:S(2)}) copy-start(f32[8,64,256]{2,1,0:T(8,128)} %head_hbm.1) | copy-start | bytes 1572868
  3.7 0.9 %copy-start.2 = (f32[16,32,128]{2,1,0:T(8,128)S(1)}, f32[16,32,128]{2,1,0:T(8,128)}, u32[]{:S(2)}) copy-start(f32[16,32,128]{2,1,0:T(8,128)} %theta_hbm.1) | copy-start | bytes 786436
  4.7 0.8 %copy-start.3 = (s32[64,256]{1,0:T(8,128)S(1)}, s32[64,256]{1,0:T(8,128)}, u32[]{:S(2)}) copy-start(s32[64,256]{1,0:T(8,128)} %soil_hbm.1) | copy-start | bytes 196612
  5.5 0.7 %copy-start.4 = (f32[32,128]{1,0:T(8,128)S(1)}, f32[32,128]{1,0:T(8,128)}, u32[]{:S(2)}) copy-start(f32[32,128]{1,0:T(8,128)} %terrain_hbm.1) | copy-start | bytes 49156

commit v2 on v1

--- a/solution.py
+++ b/solution.py
@@ -74,11 +74,10 @@
     alpha_ref,
     expo_ref,
     ksat_ref,
-    theta_out,
+    done,
     head_out,
     th,
     sw,
-    done,
     tr,
     hd,
     soil,
@@ -106,7 +105,6 @@
     bsend,
     brecv,
     local_sem,
-    out_sem,
     near_send,
     near_recv,
     g_send,
@@ -456,7 +454,7 @@
     def down(i):
         total = None
         for q in range(2):
-            term = dot(gath[pair_ref[tile_at[i], q]], tl[i, q])
+            term = dot(gath[pair_ref[q, tile_at[i]]], tl[i, q])
             total = term if total is None else total + term
         return total
 
@@ -546,8 +544,6 @@
         done[k] = value
 
     sweep_once(1, sw, store_second)
-    out_theta = pltpu.make_async_copy(done.at[1:lev], theta_out.at[1:lev], out_sem.at[0])
-    out_theta.start()
 
     def hear(index):
         @pl.when(index != me)
@@ -582,7 +578,7 @@
     def advance_head(k):
         own = (k, slice(0, height), slice(0, width))
         value = hd[own] + (c0 * vec0[own] + c1 * vec1[own] + c2 * vec2[own])
-        hd[own] = value
+        head_out[k] = value
         return value
 
     surface = advance_head(0)
@@ -598,7 +594,7 @@
         for q in range(2):
             contrib.append(
                 (
-                    pair_ref[first + i, q],
+                    pair_ref[q, first + i],
                     dot_nt(halves[:, i * LANES : (i + 1) * LANES], tl[i + 1, q]),
                 )
             )
@@ -629,10 +625,6 @@
 
     for k in range(1, levs):
         advance_head(k)
-    out_head = pltpu.make_async_copy(
-        hd.at[:, 0:height, 0:width], head_out, out_sem.at[1]
-    )
-    out_head.start()
 
     own_y = x // ratio
 
@@ -647,8 +639,6 @@
 
     each(ngx, collect)
     done[0] = done[0] + evaporate * jnp.sum(brecv[...], axis=0)
-    out_level = pltpu.make_async_copy(done.at[0], theta_out.at[0], out_sem.at[2])
-    out_level.start()
 
     for cond, what in sent:
 
@@ -681,9 +671,16 @@
                     (to_x, t),
                 ).wait_send()
 
-    out_theta.wait()
-    out_head.wait()
-    out_level.wait()
+
+def deliver(theta_ref, head_ref, theta_out, head_out, sem):
+    copies = [
+        pltpu.make_async_copy(theta_ref, theta_out, sem.at[0]),
+        pltpu.make_async_copy(head_ref, head_out, sem.at[1]),
+    ]
+    for copy in copies:
+        copy.start()
+    for copy in copies:
+        copy.wait()
 
 
 def shards(ngx, ngy, theta, terrain, head, soil, pair_map, tiles, vg_alpha, vg_n, ksat):
@@ -695,19 +692,19 @@
     ext = (levs, height + SUB, width + LANES)
     dma = pltpu.SemaphoreType.DMA
     group = ngx * ngy
-    anywhere = pl.BlockSpec(memory_space=pl.ANY)
+    anywhere = pl.BlockSpec(memory_space=pltpu.HBM)
+    whole = pl.BlockSpec(memory_space=pltpu.VMEM)
     scalars = pl.BlockSpec(memory_space=pltpu.SMEM)
     vmem = lambda *shape: pltpu.VMEM(shape, F32)
-    return pl.pallas_call(
+    results = pl.pallas_call(
         functools.partial(kernel, ngx, ngy),
         out_shape=(
             jax.ShapeDtypeStruct(theta.shape, F32),
             jax.ShapeDtypeStruct(head.shape, F32),
         ),
         in_specs=[anywhere] * 5 + [scalars] * 4,
-        out_specs=(anywhere, anywhere),
+        out_specs=(whole, whole),
         scratch_shapes=[
-            vmem(*theta.shape),
             vmem(*theta.shape),
             vmem(*theta.shape),
             vmem(*terrain.shape),
@@ -737,7 +734,6 @@
             vmem(ngy * ratio, th_rows, LANES),
             vmem(ngx, th_rows, LANES),
             dma((tile_count + 6,)),
-            dma((3,)),
             dma((10,)),
             dma((10,)),
             dma((3, ngx)),
@@ -750,10 +746,20 @@
             dma((ngx,)),
         ],
         compiler_params=pltpu.CompilerParams(
-            collective_id=0, has_side_effects=True, vmem_limit_bytes=40 * 1024 * 1024
+            collective_id=0, has_side_effects=True, vmem_limit_bytes=63 * 1024 * 1024
         ),
         name="coupled_step",
-    )(theta, terrain, head, soil, tiles, pair_map, vg_alpha, vg_n, ksat)
+    )(theta, terrain, head, soil, tiles, pair_map.T, vg_alpha, vg_n, ksat)
+    anyplace = pl.BlockSpec(memory_space=pl.ANY)
+    return pl.pallas_call(
+        deliver,
+        out_shape=tuple(jax.ShapeDtypeStruct(r.shape, F32) for r in results),
+        in_specs=[anyplace, anyplace],
+        out_specs=(anywhere, anywhere),
+        scratch_shapes=[dma((2,))],
+        compiler_params=pltpu.CompilerParams(vmem_limit_bytes=63 * 1024 * 1024),
+        name="deliver",
+    )(*results)
 
 
 def solution(mesh):

time: 35.1 us -> 53.1 us (1.51)
  Pallas kernels: 27 us -> 52.3 us
  local copies, waits for them, and re-layouts: 7.05 us -> 0 us
    pallas_call x0 -> x1, Pallas kernels: none -> 24.9 us  [shards(): pl.pallas_call(deliver, out_shape=tuple((jax.ShapeDtypeStruct(r.shape, F3...]
    unnamed x19 -> x0, local copies, waits for them, and re-layouts: 7.05 us -> none
where the time goes in v2:
time: 53.1 us; the launch traced here: 52.9 us
  Pallas kernels  52.3 us (98%)
  between operations  0.64 us (1%)
    pallas_call x1, Pallas kernels, shards(): pl.pallas_call(functools.partial(kernel, ngx, ngy), out_shape=(jax.ShapeD...  27.3 us
    pallas_call x1, Pallas kernels, shards(): pl.pallas_call(deliver, out_shape=tuple((jax.ShapeDtypeStruct(r.shape, F3...  24.9 us

profile of v2, /device:TPU:0, one launch (start us, length us, event | category | flops | bytes accessed | tf_op | source)
XLA Modules:
  0.0 52.9 jit_solution(5364470270742854006)
XLA Ops:
  0.6 27.3 %coupled_step.1 = (f32[16,32,128]{2,1,0:T(8,128)}, f32[8,64,256]{2,1,0:T(8,128)}) custom-call(f32[16,32,128]{2,1,0:T(8,128)} %theta_hbm.1, f32[32,128]{1,0:T(8,128)} %terrain_hbm.1, f32[8,64,256]{2,1,0:T(8,128)} %head_hbm.1, s32[64,256]{1,0:T(8,128)} %soil_hbm.1, f32[8,2,128,128]{3,2,1,0:T(8,128)} %tiles_hbm.1, s32[2,8]{1,0:T(2,128)} %bitcast.1, ...), custom_call_target="tpu_custom_call" | custom-call | tf_op jit(solution)/shard_map/coupled_step/pallas_call | solution.py:699
  27.9 24.9 %deliver.1 = (f32[16,32,128]{2,1,0:T(8,128)}, f32[8,64,256]{2,1,0:T(8,128)}) custom-call(f32[16,32,128]{2,1,0:T(8,128)} %get-tuple-element.4.theta_ref, f32[8,64,256]{2,1,0:T(8,128)} %get-tuple-element.5.head_ref), custom_call_target="tpu_custom_call" | custom-call | tf_op jit(solution)/shard_map/deliver/pallas_call | solution.py:754

commit v3 on v1

--- a/solution.py
+++ b/solution.py
@@ -84,12 +84,14 @@
     soil,
     soilf,
     tl,
-    rowh,
-    rows_soil,
-    pack,
-    colr,
+    rows_out,
+    rows_in,
+    cols_out,
+    cols_in,
     corner,
     gath,
+    edge_out,
+    edge_in,
     trs,
     trr,
     tcs,
@@ -151,11 +153,10 @@
     ]
     c_tiles = [load(tiles_hbm.at[tile_at[i]], tl.at[i]) for i in range(tile_count + 2)]
 
-    rowh[...] = jnp.zeros(rowh.shape, F32)
-    rows_soil[...] = jnp.zeros(rows_soil.shape, jnp.int32)
-    colr[...] = jnp.zeros(colr.shape, F32)
+    rows_in[...] = jnp.zeros(rows_in.shape, F32)
+    cols_in[...] = jnp.zeros(cols_in.shape, F32)
     corner[...] = jnp.zeros(corner.shape, F32)
-    gath[...] = jnp.zeros(gath.shape, F32)
+    edge_in[...] = jnp.zeros(edge_in.shape, F32)
     trr[...] = jnp.zeros(trr.shape, F32)
     tcr[...] = jnp.zeros(tcr.shape, F32)
 
@@ -175,19 +176,24 @@
 
     lane = lax.broadcasted_iota(jnp.int32, (1, LANES), 1)
 
-    def pack_theta(sweep, source):
-        trs[sweep, 0] = source[:, 0, :]
-        trs[sweep, 1] = source[:, th_rows - 1, :]
+    def edge_columns(source):
         first_col = jnp.zeros((th_rows, LANES), F32)
         last_col = jnp.zeros((th_rows, LANES), F32)
         for k in range(lev):
             first_col = jnp.where(lane == k, turn(source[k], k, 1), first_col)
             last_col = jnp.where(lane == k, turn(source[k], k + 1, 1), last_col)
-        tcs[sweep, 0] = first_col
-        tcs[sweep, 1] = last_col
+        return first_col, last_col
+
+    def place(chunk):
+        col = (chunk % tile_count) * LANES
+        return levs + 1 + chunk // tile_count, slice(0, SUB), slice(col, col + LANES)
 
     c_theta.wait()
-    pack_theta(0, th)
+    cols_out[0, height:] = th[:, 0, :]
+    cols_out[1, height:] = th[:, th_rows - 1, :]
+    for side, columns in enumerate(edge_columns(th)):
+        for chunk in range(th_rows // SUB):
+            rows_out[(side,) + place(chunk)] = columns[chunk * SUB : (chunk + 1) * SUB]
 
     c_head.wait()
     c_soil.wait()
@@ -201,8 +207,11 @@
             a, b = soilf[0:height, 0:LANES], soilf[0:height, width - LANES : width]
         edge_l = jnp.where(lane // 4 == k, turn(a, 4 * k, 1), edge_l)
         edge_r = jnp.where((LANES - 1 - lane) // 4 == k, turn(b, -4 * k, 1), edge_r)
-    pack[0] = edge_l
-    pack[1] = edge_r
+    cols_out[0, 0:height] = edge_l
+    cols_out[1, 0:height] = edge_r
+    for side, row in enumerate((0, height - SUB)):
+        rows_out[side, 0:levs] = hd[:, row : row + SUB, 0:width]
+        rows_out[side, levs] = soilf[row : row + SUB, 0:width]
 
     pl.semaphore_wait(barrier, group - 1)
 
@@ -236,77 +245,42 @@
         send(cond, src, dst, near_send.at[index], near_recv.at[index], to)
         near.append((cond_in, dst, near_recv.at[index]))
 
-    halo(0, left, head_hbm.at[:, 0:SUB, :], rowh.at[0], (x, y - 1), right_y)
-    halo(1, right_y, head_hbm.at[:, height - SUB :, :], rowh.at[1], (x, y + 1), left)
-    halo(2, low, pack.at[0], colr.at[0], (x - 1, y), high_x)
-    halo(3, high_x, pack.at[1], colr.at[1], (x + 1, y), low)
+    both = jnp.logical_and
+    halo(0, left, rows_out.at[0], rows_in.at[0], (x, y - 1), right_y)
+    halo(1, right_y, rows_out.at[1], rows_in.at[1], (x, y + 1), left)
+    halo(2, low, cols_out.at[0], cols_in.at[0], (x - 1, y), high_x)
+    halo(3, high_x, cols_out.at[1], cols_in.at[1], (x + 1, y), low)
 
     dest = x // ratio
     part = x % ratio
     offset = pl.multiple_of(part * th_rows, th_rows)
     body = ratio * th_rows
 
-    def spread(kind, cond, dest_y, src, dst, slot):
+    slot = y * ratio + part
+    src, dst = th.at[0], gath.at[y, pl.ds(offset, th_rows)]
+
+    def spread(act):
         def one(i):
-            me_too = jnp.logical_and(i == x, dest_y == y)
-
-            @pl.when(jnp.logical_and(cond, jnp.logical_not(me_too)))
+            @pl.when(jnp.logical_not(both(i == x, dest == y)))
             def _():
-                remote(
-                    src, dst, g_send.at[kind, i], g_recv.at[kind, slot], (i, dest_y)
-                ).start()
+                act(remote(src, dst, g_send.at[i], g_recv.at[slot], (i, dest)))
 
         each(ngx, one)
 
-        @pl.when(jnp.logical_and(cond, dest_y == y))
-        def _():
-            dst[...] = src[...]
-
-        def finish(i):
-            me_too = jnp.logical_and(i == x, dest_y == y)
-
-            @pl.when(jnp.logical_and(cond, jnp.logical_not(me_too)))
-            def _():
-                remote(
-                    src, dst, g_send.at[kind, i], g_recv.at[kind, slot], (i, dest_y)
-                ).wait_send()
-
-        return lambda: each(ngx, finish)
-
-    slot = y * ratio + part
-    at_first, at_last = part == 0, part == ratio - 1
-    finish_spread = [
-        spread(0, x >= 0, dest, th.at[0], gath.at[y, pl.ds(offset, th_rows)], slot),
-        spread(
-            1,
-            jnp.logical_and(at_first, dest > 0),
-            dest - 1,
-            th.at[0, 0:SUB],
-            gath.at[y, body : body + SUB],
-            y,
-        ),
-        spread(
-            2,
-            jnp.logical_and(at_last, dest < ngy - 1),
-            dest + 1,
-            th.at[0, th_rows - SUB : th_rows],
-            gath.at[y, body + SUB : body + 2 * SUB],
-            y,
-        ),
-    ]
-
-    halo(4, left, soil_hbm.at[0:SUB, :], rows_soil.at[0], (x, y - 1), right_y)
-    halo(5, right_y, soil_hbm.at[height - SUB :, :], rows_soil.at[1], (x, y + 1), left)
-    both = jnp.logical_and
-    halo(6, both(low, left), pack.at[0, 0:SUB], corner.at[0], (x - 1, y - 1), both(high_x, right_y))
-    halo(7, both(low, right_y), pack.at[0, height - SUB :], corner.at[1], (x - 1, y + 1), both(high_x, left))
-    halo(8, both(high_x, left), pack.at[1, 0:SUB], corner.at[2], (x + 1, y - 1), both(low, right_y))
-    halo(9, both(high_x, right_y), pack.at[1, height - SUB :], corner.at[3], (x + 1, y + 1), both(low, left))
+    spread(lambda copy: copy.start())
+
+    @pl.when(dest == y)
+    def _():
+        dst[...] = src[...]
+
+    halo(4, both(low, left), cols_out.at[0, 0:SUB], corner.at[0], (x - 1, y - 1), both(high_x, right_y))
+    halo(5, both(low, right_y), cols_out.at[0, height - SUB : height], corner.at[1], (x - 1, y + 1), both(high_x, left))
+    halo(6, both(high_x, left), cols_out.at[1, 0:SUB], corner.at[2], (x + 1, y - 1), both(low, right_y))
+    halo(7, both(high_x, right_y), cols_out.at[1, height - SUB : height], corner.at[3], (x + 1, y + 1), both(low, left))
 
     theta_in = []
 
-    def theta_halo(sweep):
-        got = []
+    def theta_halo():
         plan = (
             (low, trs, trr, 0, (x - 1, y), high_x),
             (high_x, trs, trr, 1, (x + 1, y), low),
@@ -314,18 +288,8 @@
             (right_y, tcs, tcr, 1, (x, y + 1), left),
         )
         for index, (cond, src, dst, side, to, cond_in) in enumerate(plan):
-            send(
-                cond,
-                src.at[sweep, side],
-                dst.at[sweep, side],
-                t_send.at[sweep, index],
-                t_recv.at[sweep, index],
-                to,
-            )
-            got.append((cond_in, dst.at[sweep, side], t_recv.at[sweep, index]))
-        theta_in.append(got)
-
-    theta_halo(0)
+            send(cond, src.at[side], dst.at[side], t_send.at[index], t_recv.at[index], to)
+            theta_in.append((cond_in, dst.at[side], t_recv.at[index]))
 
     def state(k, rows, cols, alpha, expo, kmax, mask):
         power, log_u, expo_m, quarter = retention(hd[k, rows, cols], alpha, expo)
@@ -347,18 +311,15 @@
     for row in range(0, height, 32):
         state_block(slice(row, row + 32), slice(0, width), None)
 
-    def sweep_once(sweep, source, store):
-        for cond, dst, sem in theta_in[sweep]:
-            arrive(cond, dst, sem)
+    def sweep_once(source, row_below, row_above, from_right, from_left, store):
         row_at = lax.broadcasted_iota(jnp.int32, (th_rows, LANES), 0)
         metric = diffuse * tr[...]
-        from_right, from_left = tcr[sweep, 0], tcr[sweep, 1]
         for k in range(lev):
             centre = source[k]
             down = jnp.where(
-                row_at == th_rows - 1, trr[sweep, 0, k : k + 1, :], turn(centre, -1, 0)
+                row_at == th_rows - 1, row_below(k), turn(centre, -1, 0)
             )
-            up = jnp.where(row_at == 0, trr[sweep, 1, k : k + 1, :], turn(centre, 1, 0))
+            up = jnp.where(row_at == 0, row_above(k), turn(centre, 1, 0))
             east = jnp.where(
                 lane == LANES - 1, turn(from_right, LANES - 1 - k, 1), turn(centre, -1, 1)
             )
@@ -374,19 +335,48 @@
     def store_first(k, value):
         sw[k] = value
 
-    c_terrain.wait()
-    sweep_once(0, th, store_first)
-    pack_theta(1, sw)
-    theta_halo(1)
-
-    for cond, dst, sem in near:
+    first_half = lane < LANES // 2
+    for r in range(ratio):
+
+        def one(b, r=r):
+            @pl.when(jnp.logical_not(both(y * ratio + r == x, b == y)))
+            def _():
+                arrived = gath.at[b, r * th_rows : (r + 1) * th_rows]
+                remote(
+                    arrived, arrived, near_send.at[0], g_recv.at[b * ratio + r], (x, y)
+                ).wait_recv()
+
+        each(nblock, one)
+    for copy in c_tiles:
+        copy.wait()
+    grow_to = lax.broadcasted_iota(jnp.int32, (height, body), 0)
+    grow_from = lax.broadcasted_iota(jnp.int32, (height, body), 1)
+    grow = jnp.where(grow_from == grow_to // 2, infiltrate, 0.0).astype(F32)
+
+    def down(i):
+        total = None
+        for q in range(2):
+            term = dot(gath[pair_ref[q, tile_at[i]]], tl[i, q])
+            total = term if total is None else total + term
+        return total
+
+    blocks = [down(i + 1) for i in range(tile_count)]
+    blocks.append(jnp.where(first_half, down(tile_count + 1), down(0)))
+    infil = dot(grow, jnp.concatenate(blocks, axis=1))
+    edge_out[0] = infil[0:SUB]
+    edge_out[1] = infil[height - SUB : height]
+    vec0[0, 0:height] = infil
+    edges_here = len(near)
+    halo(8, left, edge_out.at[0], edge_in.at[0], (x, y - 1), right_y)
+    halo(9, right_y, edge_out.at[1], edge_in.at[1], (x, y + 1), left)
+
+    for cond, dst, sem in near[:edges_here]:
         arrive(cond, dst, sem)
     upper = lax.broadcasted_iota(jnp.int32, (SUB, 1), 0) < 4
-    first_half = lane < LANES // 2
     for k in range(levs):
-        hd[k, height:ext_h, 0:width] = jnp.where(upper, rowh[0, k], rowh[1, k])
-    soilf[height:ext_h, 0:width] = jnp.where(upper, rows_soil[0], rows_soil[1]).astype(F32)
-    right_side, left_side = colr[0], colr[1]
+        hd[k, height:ext_h, 0:width] = jnp.where(upper, rows_in[0, k], rows_in[1, k])
+    soilf[height:ext_h, 0:width] = jnp.where(upper, rows_in[0, levs], rows_in[1, levs])
+    right_side, left_side = cols_in[0, 0:height], cols_in[1, 0:height]
     right_corner = jnp.where(upper, corner[0], corner[1])
     left_corner = jnp.where(upper, corner[2], corner[3])
     for k in range(levs + 1):
@@ -415,54 +405,26 @@
         slice(height, ext_h), slice(width, ext_w), jnp.logical_and(row_ok, col_ok)
     )
 
-    def arrive_blocks(kind, cond, from_x, dst_of, slot_of):
-        def one(b):
-            mine = jnp.logical_and(from_x == x, b == y)
-
-            @pl.when(jnp.logical_and(cond, jnp.logical_not(mine)))
-            def _():
-                dst = dst_of(b)
-                remote(dst, dst, near_send.at[0], g_recv.at[kind, slot_of(b)], (x, y)).wait_recv()
-
-        each(nblock, one)
-
-    for r in range(ratio):
-        arrive_blocks(
-            0,
-            x >= 0,
-            y * ratio + r,
-            lambda b, r=r: gath.at[b, r * th_rows : (r + 1) * th_rows],
-            lambda b, r=r: b * ratio + r,
-        )
-    arrive_blocks(
-        1, right_y, (y + 1) * ratio, lambda b: gath.at[b, body : body + SUB], lambda b: b
-    )
-    arrive_blocks(
-        2,
-        left,
-        y * ratio - 1,
-        lambda b: gath.at[b, body + SUB : body + 2 * SUB],
-        lambda b: b,
-    )
-    for copy in c_tiles:
-        copy.wait()
-    grow_to = lax.broadcasted_iota(jnp.int32, (ext_h, body + 2 * SUB), 0)
-    grow_from = lax.broadcasted_iota(jnp.int32, (ext_h, body + 2 * SUB), 1)
-    source_row = jnp.where(
-        grow_to < height + 4, grow_to // 2, body + 2 * SUB - 2 + (grow_to - height - 4) // 2
-    )
-    grow = jnp.where(grow_from == source_row, infiltrate, 0.0).astype(F32)
-
-    def down(i):
-        total = None
-        for q in range(2):
-            term = dot(gath[pair_ref[tile_at[i], q]], tl[i, q])
-            total = term if total is None else total + term
-        return total
-
-    infil = [dot(grow, down(i + 1)) for i in range(tile_count)]
-    ends = jnp.where(first_half, down(tile_count + 1), down(0))
-    infil.append(dot(grow, ends))
+    def store_first(k, value):
+        sw[k] = value
+
+    def edge_column(side):
+        pieces = [rows_in[(side,) + place(chunk)] for chunk in range(th_rows // SUB)]
+        return jnp.concatenate(pieces, axis=0)
+
+    c_terrain.wait()
+    sweep_once(
+        th,
+        lambda k: cols_in[0, height + k : height + k + 1],
+        lambda k: cols_in[1, height + k : height + k + 1],
+        edge_column(0),
+        edge_column(1),
+        store_first,
+    )
+    trs[0] = sw[:, 0, :]
+    trs[1] = sw[:, th_rows - 1, :]
+    tcs[0], tcs[1] = edge_columns(sw)
+    theta_halo()
 
     def across(value):
         return (turn(value, 1, 1) + turn(value, -1, 1)) + (
@@ -479,7 +441,7 @@
 
     for k in range(levs):
         wvec[0, k] = root[k] * hd[k]
-    for k in range(levs):
+    for k in reversed(range(levs)):
         centre = root[k]
         span = around(root, k)
         flow = around(wvec.at[0], k) - span * hd[k]
@@ -489,7 +451,10 @@
             flow = flow + root[k + 1]
         rhs = centre * flow
         if k == 0:
-            rhs = rhs + jnp.concatenate(infil, axis=1)
+            for cond, dst, sem in near[edges_here:]:
+                arrive(cond, dst, sem)
+            edge = jnp.where(upper, edge_in[0], edge_in[1])
+            rhs = rhs + jnp.concatenate([vec0[0, 0:height], edge], axis=0)
         diag[k] = cap[k] + centre * span
         vec0[k] = rhs
         wvec[1, k] = centre * rhs
@@ -542,10 +507,27 @@
 
     each(group, tell)
 
+    for cond, what in sent:
+
+        @pl.when(cond)
+        def _():
+            remote(*what).wait_send()
+
+    spread(lambda copy: copy.wait_send())
+    for cond, dst, sem in theta_in:
+        arrive(cond, dst, sem)
+
     def store_second(k, value):
         done[k] = value
 
-    sweep_once(1, sw, store_second)
+    sweep_once(
+        sw,
+        lambda k: trr[0, k : k + 1],
+        lambda k: trr[1, k : k + 1],
+        tcr[0],
+        tcr[1],
+        store_second,
+    )
     out_theta = pltpu.make_async_copy(done.at[1:lev], theta_out.at[1:lev], out_sem.at[0])
     out_theta.start()
 
@@ -598,7 +580,7 @@
         for q in range(2):
             contrib.append(
                 (
-                    pair_ref[first + i, q],
+                    pair_ref[q, first + i],
                     dot_nt(halves[:, i * LANES : (i + 1) * LANES], tl[i + 1, q]),
                 )
             )
@@ -629,35 +611,9 @@
 
     for k in range(1, levs):
         advance_head(k)
-    out_head = pltpu.make_async_copy(
-        hd.at[:, 0:height, 0:width], head_out, out_sem.at[1]
-    )
+
+    out_head = pltpu.make_async_copy(hd.at[:, 0:height, 0:width], head_out, out_sem.at[1])
     out_head.start()
-
-    own_y = x // ratio
-
-    def collect(index):
-        mine = jnp.logical_and(index == x, own_y == y)
-
-        @pl.when(jnp.logical_not(mine))
-        def _():
-            remote(
-                brecv.at[index], brecv.at[index], near_send.at[0], b_recv.at[index], (x, y)
-            ).wait_recv()
-
-    each(ngx, collect)
-    done[0] = done[0] + evaporate * jnp.sum(brecv[...], axis=0)
-    out_level = pltpu.make_async_copy(done.at[0], theta_out.at[0], out_sem.at[2])
-    out_level.start()
-
-    for cond, what in sent:
-
-        @pl.when(cond)
-        def _():
-            remote(*what).wait_send()
-
-    for finish in finish_spread:
-        finish()
 
     def told(index):
         @pl.when(index != me)
@@ -667,6 +623,23 @@
             ).wait_send()
 
     each(group, told)
+
+    own_y = x // ratio
+
+    def collect(index):
+        mine = jnp.logical_and(index == x, own_y == y)
+
+        @pl.when(jnp.logical_not(mine))
+        def _():
+            remote(
+                brecv.at[index], brecv.at[index], near_send.at[0], b_recv.at[index], (x, y)
+            ).wait_recv()
+
+    each(ngx, collect)
+    done[0] = done[0] + evaporate * jnp.sum(brecv[...], axis=0)
+
+    out_level = pltpu.make_async_copy(done.at[0], theta_out.at[0], out_sem.at[2])
+    out_level.start()
     for t in range(nblock):
         for r in range(ratio):
             to_x = y * ratio + r
@@ -692,10 +665,11 @@
     body = height // 2
     ratio = body // th_rows
     tile_count = width // LANES
+    slabs = levs + 1 + pl.cdiv(th_rows // SUB, tile_count)
     ext = (levs, height + SUB, width + LANES)
     dma = pltpu.SemaphoreType.DMA
     group = ngx * ngy
-    anywhere = pl.BlockSpec(memory_space=pl.ANY)
+    anywhere = pl.BlockSpec(memory_space=pltpu.HBM)
     scalars = pl.BlockSpec(memory_space=pltpu.SMEM)
     vmem = lambda *shape: pltpu.VMEM(shape, F32)
     return pl.pallas_call(
@@ -715,16 +689,18 @@
             pltpu.VMEM((height, width), jnp.int32),
             vmem(*ext[1:]),
             vmem(tile_count + 2, 2, LANES, LANES),
-            vmem(2, levs, SUB, width),
-            pltpu.VMEM((2, SUB, width), jnp.int32),
-            vmem(2, height, LANES),
-            vmem(2, height, LANES),
+            vmem(2, slabs, SUB, width),
+            vmem(2, slabs, SUB, width),
+            vmem(2, height + lev, LANES),
+            vmem(2, height + lev, LANES),
             vmem(4, SUB, LANES),
-            vmem(ngy, body + 2 * SUB, LANES),
-            vmem(2, 2, lev, LANES),
-            vmem(2, 2, lev, LANES),
-            vmem(2, 2, th_rows, LANES),
-            vmem(2, 2, th_rows, LANES),
+            vmem(ngy, body, LANES),
+            vmem(2, SUB, width + LANES),
+            vmem(2, SUB, width + LANES),
+            vmem(2, lev, LANES),
+            vmem(2, lev, LANES),
+            vmem(2, th_rows, LANES),
+            vmem(2, th_rows, LANES),
             vmem(*ext),
             vmem(*ext),
             vmem(*ext),
@@ -740,20 +716,20 @@
             dma((3,)),
             dma((10,)),
             dma((10,)),
-            dma((3, ngx)),
-            dma((3, ngy * ratio)),
-            dma((2, 4)),
-            dma((2, 4)),
+            dma((ngx,)),
+            dma((ngy * ratio,)),
+            dma((4,)),
+            dma((4,)),
             dma((group,)),
             dma((group,)),
             dma((ngy * ratio,)),
             dma((ngx,)),
         ],
         compiler_params=pltpu.CompilerParams(
-            collective_id=0, has_side_effects=True, vmem_limit_bytes=40 * 1024 * 1024
+            collective_id=0, has_side_effects=True, vmem_limit_bytes=63 * 1024 * 1024
         ),
         name="coupled_step",
-    )(theta, terrain, head, soil, tiles, pair_map, vg_alpha, vg_n, ksat)
+    )(theta, terrain, head, soil, tiles, pair_map.T, vg_alpha, vg_n, ksat)
 
 
 def solution(mesh):

time: 35.1 us -> 29.9 us (0.85)
  local copies, waits for them, and re-layouts: 7.05 us -> 2.53 us
  Pallas kernels: 27 us -> 26.6 us
    unnamed x19 -> x4, local copies, waits for them, and re-layouts: 7.05 us -> 2.53 us
    pallas_call x1, Pallas kernels: 27 us -> 26.6 us  [shards(): pl.pallas_call(functools.partial(kernel, ngx, ngy), out_shape=(jax.ShapeD...]
where the time goes in v3:
time: 29.9 us; the launch traced here: 29.7 us
  Pallas kernels  26.6 us (89%)
  local copies, waits for them, and re-layouts  2.53 us (8%)
  between operations  0.65 us (2%)
    pallas_call x1, Pallas kernels, shards(): pl.pallas_call(functools.partial(kernel, ngx, ngy), out_shape=(jax.ShapeD...  26.6 us
    unnamed x4, local copies, waits for them, and re-layouts  2.53 us

profile of v3, /device:TPU:0, one launch (start us, length us, event | category | flops | bytes accessed | tf_op | source)
XLA Modules:
  0.0 29.7 jit_solution(7848454957781236666)
XLA Ops:
  0.6 26.6 %coupled_step.1 = (f32[16,32,128]{2,1,0:T(8,128)}, f32[8,64,256]{2,1,0:T(8,128)}) custom-call(f32[16,32,128]{2,1,0:T(8,128)} %theta_hbm.1, f32[32,128]{1,0:T(8,128)} %terrain_hbm.1, f32[8,64,256]{2,1,0:T(8,128)} %head_hbm.1, s32[64,256]{1,0:T(8,128)} %soil_hbm.1, f32[8,2,128,128]{3,2,1,0:T(8,128)} %tiles_hbm.1, s32[2,8]{1,0:T(2,128)} %bitcast.1, ...), custom_call_target="tpu_custom_call" | custom-call | tf_op jit(solution)/shard_map/coupled_step/pallas_call | solution.py:675
  27.2 0.0 copy-start
  27.2 1.7 %copy.13 = f32[16,32,128]{2,1,0:T(8,128)} copy(f32[16,32,128]{2,1,0:T(8,128)} %get-tuple-element.4) | data formatting | bytes 524288
  28.9 0.0 copy-done
  28.9 0.8 %copy.14 = f32[8,64,256]{2,1,0:T(8,128)} copy(f32[8,64,256]{2,1,0:T(8,128)S(1)} %copy-done) | data formatting | bytes 1048576
Async XLA Ops:
  27.2 1.7 %copy-start = (f32[8,64,256]{2,1,0:T(8,128)S(1)}, f32[8,64,256]{2,1,0:T(8,128)}, u32[]{:S(2)}) copy-start(f32[8,64,256]{2,1,0:T(8,128)} %get-tuple-element.5) | copy-start | bytes 1572868

commit v4 on v3

--- a/solution.py
+++ b/solution.py
@@ -184,9 +184,12 @@
             last_col = jnp.where(lane == k, turn(source[k], k + 1, 1), last_col)
         return first_col, last_col
 
+    pairs = levs // 2 + 1
+    upper = lax.broadcasted_iota(jnp.int32, (SUB, 1), 0) < 4
+
     def place(chunk):
         col = (chunk % tile_count) * LANES
-        return levs + 1 + chunk // tile_count, slice(0, SUB), slice(col, col + LANES)
+        return pairs + chunk // tile_count, slice(0, SUB), slice(col, col + LANES)
 
     c_theta.wait()
     cols_out[0, height:] = th[:, 0, :]
@@ -210,8 +213,17 @@
     cols_out[0, 0:height] = edge_l
     cols_out[1, 0:height] = edge_r
     for side, row in enumerate((0, height - SUB)):
-        rows_out[side, 0:levs] = hd[:, row : row + SUB, 0:width]
-        rows_out[side, levs] = soilf[row : row + SUB, 0:width]
+        for p in range(pairs):
+            if p < levs // 2:
+                even = hd[2 * p, row : row + SUB, 0:width]
+                odd = hd[2 * p + 1, row : row + SUB, 0:width]
+            else:
+                even = odd = soilf[row : row + SUB, 0:width]
+            if side == 0:
+                odd = turn(odd, 4, 0)
+            else:
+                even = turn(even, 4, 0)
+            rows_out[side, p] = jnp.where(upper, even, odd)
 
     pl.semaphore_wait(barrier, group - 1)
 
@@ -370,12 +382,19 @@
     halo(8, left, edge_out.at[0], edge_in.at[0], (x, y - 1), right_y)
     halo(9, right_y, edge_out.at[1], edge_in.at[1], (x, y + 1), left)
 
+    def rows_beside(k):
+        below, above = rows_in[0, k // 2], rows_in[1, k // 2]
+        if k % 2 == 0:
+            above = turn(above, 4, 0)
+        else:
+            below = turn(below, 4, 0)
+        return jnp.where(upper, below, above)
+
     for cond, dst, sem in near[:edges_here]:
         arrive(cond, dst, sem)
-    upper = lax.broadcasted_iota(jnp.int32, (SUB, 1), 0) < 4
     for k in range(levs):
-        hd[k, height:ext_h, 0:width] = jnp.where(upper, rows_in[0, k], rows_in[1, k])
-    soilf[height:ext_h, 0:width] = jnp.where(upper, rows_in[0, levs], rows_in[1, levs])
+        hd[k, height:ext_h, 0:width] = rows_beside(k)
+    soilf[height:ext_h, 0:width] = rows_beside(levs)
     right_side, left_side = cols_in[0, 0:height], cols_in[1, 0:height]
     right_corner = jnp.where(upper, corner[0], corner[1])
     left_corner = jnp.where(upper, corner[2], corner[3])
@@ -404,27 +423,6 @@
     state_block(
         slice(height, ext_h), slice(width, ext_w), jnp.logical_and(row_ok, col_ok)
     )
-
-    def store_first(k, value):
-        sw[k] = value
-
-    def edge_column(side):
-        pieces = [rows_in[(side,) + place(chunk)] for chunk in range(th_rows // SUB)]
-        return jnp.concatenate(pieces, axis=0)
-
-    c_terrain.wait()
-    sweep_once(
-        th,
-        lambda k: cols_in[0, height + k : height + k + 1],
-        lambda k: cols_in[1, height + k : height + k + 1],
-        edge_column(0),
-        edge_column(1),
-        store_first,
-    )
-    trs[0] = sw[:, 0, :]
-    trs[1] = sw[:, th_rows - 1, :]
-    tcs[0], tcs[1] = edge_columns(sw)
-    theta_halo()
 
     def across(value):
         return (turn(value, 1, 1) + turn(value, -1, 1)) + (
@@ -507,29 +505,34 @@
 
     each(group, tell)
 
-    for cond, what in sent:
+    near_count = len(sent)
+    for cond, what in sent[:near_count]:
 
         @pl.when(cond)
         def _():
             remote(*what).wait_send()
 
     spread(lambda copy: copy.wait_send())
-    for cond, dst, sem in theta_in:
-        arrive(cond, dst, sem)
-
-    def store_second(k, value):
-        done[k] = value
-
+    def store_first(k, value):
+        sw[k] = value
+
+    def edge_column(side):
+        pieces = [rows_in[(side,) + place(chunk)] for chunk in range(th_rows // SUB)]
+        return jnp.concatenate(pieces, axis=0)
+
+    c_terrain.wait()
     sweep_once(
-        sw,
-        lambda k: trr[0, k : k + 1],
-        lambda k: trr[1, k : k + 1],
-        tcr[0],
-        tcr[1],
-        store_second,
-    )
-    out_theta = pltpu.make_async_copy(done.at[1:lev], theta_out.at[1:lev], out_sem.at[0])
-    out_theta.start()
+        th,
+        lambda k: cols_in[0, height + k : height + k + 1],
+        lambda k: cols_in[1, height + k : height + k + 1],
+        edge_column(0),
+        edge_column(1),
+        store_first,
+    )
+    trs[0] = sw[:, 0, :]
+    trs[1] = sw[:, th_rows - 1, :]
+    tcs[0], tcs[1] = edge_columns(sw)
+    theta_halo()
 
     def hear(index):
         @pl.when(index != me)
@@ -624,6 +627,29 @@
 
     each(group, told)
 
+    for cond, dst, sem in theta_in:
+        arrive(cond, dst, sem)
+
+    def store_second(k, value):
+        done[k] = value
+
+    sweep_once(
+        sw,
+        lambda k: trr[0, k : k + 1],
+        lambda k: trr[1, k : k + 1],
+        tcr[0],
+        tcr[1],
+        store_second,
+    )
+    out_theta = pltpu.make_async_copy(done.at[1:lev], theta_out.at[1:lev], out_sem.at[0])
+    out_theta.start()
+
+    for cond, what in sent[near_count:]:
+
+        @pl.when(cond)
+        def _():
+            remote(*what).wait_send()
+
     own_y = x // ratio
 
     def collect(index):
@@ -665,7 +691,7 @@
     body = height // 2
     ratio = body // th_rows
     tile_count = width // LANES
-    slabs = levs + 1 + pl.cdiv(th_rows // SUB, tile_count)
+    slabs = levs // 2 + 1 + pl.cdiv(th_rows // SUB, tile_count)
     ext = (levs, height + SUB, width + LANES)
     dma = pltpu.SemaphoreType.DMA
     group = ngx * ngy

time: 29.9 us -> 29.2 us (0.977)
  Pallas kernels: 26.6 us -> 25.8 us
    pallas_call x1, Pallas kernels: 26.6 us -> 25.8 us  [shards(): pl.pallas_call(functools.partial(kernel, ngx, ngy), out_shape=(jax.ShapeD...]
where the time goes in v4:
time: 29.2 us; the launch traced here: 29 us
  Pallas kernels  25.8 us (88%)
  local copies, waits for them, and re-layouts  2.53 us (9%)
  between operations  0.65 us (2%)
    pallas_call x1, Pallas kernels, shards(): pl.pallas_call(functools.partial(kernel, ngx, ngy), out_shape=(jax.ShapeD...  25.8 us
    unnamed x4, local copies, waits for them, and re-layouts  2.53 us

profile of v4, /device:TPU:0, one launch (start us, length us, event | category | flops | bytes accessed | tf_op | source)
XLA Modules:
  0.0 29.0 jit_solution(9951826670620157673)
XLA Ops:
  0.6 25.8 %coupled_step.1 = (f32[16,32,128]{2,1,0:T(8,128)}, f32[8,64,256]{2,1,0:T(8,128)}) custom-call(f32[16,32,128]{2,1,0:T(8,128)} %theta_hbm.1, f32[32,128]{1,0:T(8,128)} %terrain_hbm.1, f32[8,64,256]{2,1,0:T(8,128)} %head_hbm.1, s32[64,256]{1,0:T(8,128)} %soil_hbm.1, f32[8,2,128,128]{3,2,1,0:T(8,128)} %tiles_hbm.1, s32[2,8]{1,0:T(2,128)} %bitcast.1, ...), custom_call_target="tpu_custom_call" | custom-call | tf_op jit(solution)/shard_map/coupled_step/pallas_call | solution.py:701
  26.5 0.0 copy-start
  26.5 1.7 %copy.13 = f32[16,32,128]{2,1,0:T(8,128)} copy(f32[16,32,128]{2,1,0:T(8,128)} %get-tuple-element.4) | data formatting | bytes 524288
  28.2 0.0 copy-done
  28.2 0.8 %copy.14 = f32[8,64,256]{2,1,0:T(8,128)} copy(f32[8,64,256]{2,1,0:T(8,128)S(1)} %copy-done) | data formatting | bytes 1048576
Async XLA Ops:
  26.5 1.7 %copy-start = (f32[8,64,256]{2,1,0:T(8,128)S(1)}, f32[8,64,256]{2,1,0:T(8,128)}, u32[]{:S(2)}) copy-start(f32[8,64,256]{2,1,0:T(8,128)} %get-tuple-element.5) | copy-start | bytes 1572868

commit v5 on v4

--- a/solution.py
+++ b/solution.py
@@ -493,17 +493,39 @@
     packed = jnp.zeros((SUB, LANES), F32)
     for index, value in enumerate(sums):
         packed = jnp.where(row8 == index, jnp.sum(value, axis=0, keepdims=True), packed)
-    mom[...] = packed
-    momr[me] = packed
-
-    def tell(index):
-        @pl.when(index != me)
-        def _():
-            remote(
-                mom, momr.at[me], m_send.at[index], m_recv.at[me], (index // ngy, index % ngy)
-            ).start()
-
-    each(group, tell)
+    def line(stage, count, at, to, act):
+        def one(index):
+            @pl.when(index != at)
+            def _():
+                act(
+                    remote(
+                        mom.at[stage],
+                        momr.at[stage, at],
+                        m_send.at[stage, index],
+                        m_recv.at[stage, at],
+                        to(index),
+                    )
+                )
+
+        each(count, one)
+
+    def hear(stage, count, at):
+        def one(index):
+            @pl.when(index != at)
+            def _():
+                arrived = momr.at[stage, index]
+                remote(
+                    arrived, arrived, near_send.at[0], m_recv.at[stage, index], (x, y)
+                ).wait_recv()
+
+        each(count, one)
+        return jnp.sum(momr[stage, 0:count], axis=0)
+
+    along_y = (0, ngy, y, lambda index: (x, index))
+    along_x = (1, ngx, x, lambda index: (index, y))
+    mom[0] = packed
+    momr[0, y] = packed
+    line(*along_y, lambda copy: copy.start())
 
     near_count = len(sent)
     for cond, what in sent[:near_count]:
@@ -534,13 +556,11 @@
     tcs[0], tcs[1] = edge_columns(sw)
     theta_halo()
 
-    def hear(index):
-        @pl.when(index != me)
-        def _():
-            remote(mom, momr.at[index], near_send.at[0], m_recv.at[index], (x, y)).wait_recv()
-
-    each(group, hear)
-    moments = jnp.sum(jnp.sum(momr[...], axis=0), axis=1, keepdims=True)
+    subtotal = hear(0, ngy, y)
+    mom[1] = subtotal
+    momr[1, x] = subtotal
+    line(*along_x, lambda copy: copy.start())
+    moments = jnp.sum(hear(1, ngx, x), axis=1, keepdims=True)
     mu = [moments[i : i + 1, :] for i in range(6)]
     scale = mu[1] / mu[0]
     inverse = mu[0] / mu[1]
@@ -618,14 +638,8 @@
     out_head = pltpu.make_async_copy(hd.at[:, 0:height, 0:width], head_out, out_sem.at[1])
     out_head.start()
 
-    def told(index):
-        @pl.when(index != me)
-        def _():
-            remote(
-                mom, momr.at[me], m_send.at[index], m_recv.at[me], (index // ngy, index % ngy)
-            ).wait_send()
-
-    each(group, told)
+    line(*along_y, lambda copy: copy.wait_send())
+    line(*along_x, lambda copy: copy.wait_send())
 
     for cond, dst, sem in theta_in:
         arrive(cond, dst, sem)
@@ -694,7 +708,6 @@
     slabs = levs // 2 + 1 + pl.cdiv(th_rows // SUB, tile_count)
     ext = (levs, height + SUB, width + LANES)
     dma = pltpu.SemaphoreType.DMA
-    group = ngx * ngy
     anywhere = pl.BlockSpec(memory_space=pltpu.HBM)
     scalars = pl.BlockSpec(memory_space=pltpu.SMEM)
     vmem = lambda *shape: pltpu.VMEM(shape, F32)
@@ -734,8 +747,8 @@
             vmem(*ext),
             vmem(*ext),
             vmem(2, *ext),
-            vmem(SUB, LANES),
-            vmem(group, SUB, LANES),
+            vmem(2, SUB, LANES),
+            vmem(2, max(ngx, ngy), SUB, LANES),
             vmem(ngy * ratio, th_rows, LANES),
             vmem(ngx, th_rows, LANES),
             dma((tile_count + 6,)),
@@ -746,8 +759,8 @@
             dma((ngy * ratio,)),
             dma((4,)),
             dma((4,)),
-            dma((group,)),
-            dma((group,)),
+            dma((2, max(ngx, ngy))),
+            dma((2, max(ngx, ngy))),
             dma((ngy * ratio,)),
             dma((ngx,)),
         ],

time: 29.2 us -> 31 us (1.062)
  Pallas kernels: 25.8 us -> 27.6 us
    pallas_call x1, Pallas kernels: 25.8 us -> 27.6 us  [shards(): pl.pallas_call(functools.partial(kernel, ngx, ngy), out_shape=(jax.ShapeD...]
where the time goes in v5:
time: 31 us; the launch traced here: 30.8 us
  Pallas kernels  27.6 us (89%)
  local copies, waits for them, and re-layouts  2.53 us (8%)
  between operations  0.65 us (2%)
    pallas_call x1, Pallas kernels, shards(): pl.pallas_call(functools.partial(kernel, ngx, ngy), out_shape=(jax.ShapeD...  27.6 us
    unnamed x4, local copies, waits for them, and re-layouts  2.53 us

profile of v5, /device:TPU:0, one launch (start us, length us, event | category | flops | bytes accessed | tf_op | source)
XLA Modules:
  0.0 30.8 jit_solution(11797591116783991524)
XLA Ops:
  0.6 27.6 %coupled_step.1 = (f32[16,32,128]{2,1,0:T(8,128)}, f32[8,64,256]{2,1,0:T(8,128)}) custom-call(f32[16,32,128]{2,1,0:T(8,128)} %theta_hbm.1, f32[32,128]{1,0:T(8,128)} %terrain_hbm.1, f32[8,64,256]{2,1,0:T(8,128)} %head_hbm.1, s32[64,256]{1,0:T(8,128)} %soil_hbm.1, f32[8,2,128,128]{3,2,1,0:T(8,128)} %tiles_hbm.1, s32[2,8]{1,0:T(2,128)} %bitcast.1, ...), custom_call_target="tpu_custom_call" | custom-call | tf_op jit(solution)/shard_map/coupled_step/pallas_call | solution.py:714
  28.2 0.0 copy-start
  28.2 1.7 %copy.13 = f32[16,32,128]{2,1,0:T(8,128)} copy(f32[16,32,128]{2,1,0:T(8,128)} %get-tuple-element.4) | data formatting | bytes 524288
  30.0 0.0 copy-done
  30.0 0.8 %copy.14 = f32[8,64,256]{2,1,0:T(8,128)} copy(f32[8,64,256]{2,1,0:T(8,128)S(1)} %copy-done) | data formatting | bytes 1048576
Async XLA Ops:
  28.2 1.7 %copy-start = (f32[8,64,256]{2,1,0:T(8,128)S(1)}, f32[8,64,256]{2,1,0:T(8,128)}, u32[]{:S(2)}) copy-start(f32[8,64,256]{2,1,0:T(8,128)} %get-tuple-element.5) | copy-start | bytes 1572868
